TPU v7x, 32 devices: a whole 2x2x4 slice. The times are simulated.
32 devices in a mesh: seq: 16 (over z, y, x), tp: 2 (over core).
Axes of the slice: x: 2, y: 2, z: 4, core: 2. Of those that a mesh axis runs over, the one named last changes fastest.
Arguments:
- byte_states: bfloat16 [2, 4096, 1024], P(None, 'seq'), may hold values from -6 to 6
- lengths: int32 [2], replicated, may hold values from 512 to 2048, as said below
- w_patch: bfloat16 [1024, 8192], P(None, 'tp'), may hold values from -0.0625 to 0.0625
- norm_global: bfloat16 [1024], replicated, may hold values from 0.5 to 1.5
- w_in: bfloat16 [1024, 4640], P(None, 'tp'), may hold values from -0.1875 to 0.1875
- conv_w: bfloat16 [4, 2560], P(None, 'tp'), may hold values from -3 to 3
- conv_b: bfloat16 [2560], P('tp'), may hold values from -0.5 to 0.5
- dt_bias: bfloat16 [32], P('tp'), may hold values from -3 to -1
- a_log: bfloat16 [32], P('tp'), may hold values from -12 to 0
- d_skip: bfloat16 [32], P('tp'), may hold values from 0.5 to 1.5
- mix_gain: bfloat16 [2048], P('tp'), may hold values from 0.5 to 1.5
- w_out: bfloat16 [1024, 2048], P(None, 'tp'), may hold values from -0.125 to 0.125
- norm_attn: bfloat16 [1024], replicated, may hold values from 0.5 to 1.5
- w_qkv: bfloat16 [1024, 3072], P(None, 'tp'), may hold values from -0.1875 to 0.1875
- w_o: bfloat16 [1024, 1024], P(None, 'tp'), may hold values from -0.375 to 0.375
- norm_mlp: bfloat16 [1024], replicated, may hold values from 0.5 to 1.5
- w_gate: bfloat16 [1024, 4096], P(None, 'tp'), may hold values from -0.1875 to 0.1875
- w_up: bfloat16 [1024, 4096], P(None, 'tp'), may hold values from -0.1875 to 0.1875
- w_down: bfloat16 [1024, 4096], P(None, 'tp'), may hold values from -0.09375 to 0.09375
- w_head: bfloat16 [1024, 256], P(None, 'tp'), may hold values from -0.1875 to 0.1875
- d_logits: bfloat16 [2, 4096, 256], P(None, 'seq', 'tp'), may hold values from -6 to 6
Outputs:
- logits: float32 [2, 4096, 256], P(None, 'seq', 'tp')
- grad_bytes: float32 [2, 4096, 1024], P(None, 'seq', 'tp')
- grad_w_patch: float32 [1024, 8192], P('seq', 'tp')
- grad_norm_global: float32 [1024], replicated
- grad_w_in: float32 [1024, 4640], P('seq', 'tp')
- grad_conv_w: float32 [4, 2560], P(None, 'tp')
- grad_conv_b: float32 [2560], P('tp')
- grad_dt_bias: float32 [32], P('tp')
- grad_a_log: float32 [32], P('tp')
- grad_d_skip: float32 [32], P('tp')
- grad_mix_gain: float32 [2048], P('tp')
- grad_w_out: float32 [1024, 2048], P('seq', 'tp')
- grad_norm_attn: float32 [1024], replicated
- grad_w_qkv: float32 [1024, 3072], P('seq', 'tp')
- grad_w_o: float32 [1024, 1024], P('seq', 'tp')
- grad_norm_mlp: float32 [1024], replicated
- grad_w_gate: float32 [1024, 4096], P('seq', 'tp')
- grad_w_up: float32 [1024, 4096], P('seq', 'tp')
- grad_w_down: float32 [1024, 4096], P('seq', 'tp')
- grad_w_head: float32 [1024, 256], P('seq', 'tp')
Inputs may be any that keep to these rules, and one draw needn't show every extreme that they name: `lengths`: each length is a multiple of 8, and one equals 2048.
All inputs are finite; a program needn't handle non-finite values.
Results may differ from a plain program's by a relative error of at most 0.019.
Values sent between devices are 32-bit elements; how exact they have to be, the bound alone decides.
No kernel may reach another device: no remote copies, remote signals or barrier semaphores. Data moves between devices by JAX's collectives and lax.ppermute only.
A program may use at most 320 MiB of HBM per device.

v0:
```python
from functools import partial

import jax
import jax.numpy as jnp
from jax import lax
from jax.experimental import pallas as pl
from jax.experimental.pallas import tpu as pltpu
from jax.sharding import PartitionSpec as P

NS = 128
AD = 64
QUAD = 4


NO_COST = pl.CostEstimate(flops=1024, bytes_accessed=1024, transcendentals=0)
ROOMY = pltpu.CompilerParams(vmem_limit_bytes=56 * 1024 * 1024)

epsilon = 1e-05
highest = lax.Precision.HIGHEST
masked_score = -1e30


def dot_plain(left_side, right_side):
    return jnp.dot(left_side, right_side, preferred_element_type=jnp.float32)


def dot_trans(left_side, right_side):
    return lax.dot_general(
        left_side, right_side, (((1,), (1,)), ((), ())), preferred_element_type=jnp.float32
    )


def dot_left(left_side, right_side):
    return lax.dot_general(
        left_side, right_side, (((0,), (0,)), ((), ())), preferred_element_type=jnp.float32
    )


def rms_scale(values):
    return lax.rsqrt(jnp.mean(values * values, axis=-1, keepdims=True) + epsilon)


def hidden_parts(mlp_in, grad_hidden, w_gate, w_up):
    gate_proj = dot_plain(mlp_in, w_gate)
    up_proj = dot_plain(mlp_in, w_up)
    sigmoid_gate = jax.nn.sigmoid(gate_proj)
    hidden_low = (gate_proj * sigmoid_gate * up_proj).astype(jnp.bfloat16)
    grad_gate_low = (
        grad_hidden * up_proj * sigmoid_gate * (1.0 + gate_proj * (1.0 - sigmoid_gate))
    ).astype(jnp.bfloat16)
    grad_up_low = (grad_hidden * gate_proj * sigmoid_gate).astype(jnp.bfloat16)
    return (hidden_low, grad_gate_low, grad_up_low)


def rms_back(values, gain_values, grad_out):
    scale = rms_scale(values)
    scaled = gain_values * grad_out
    inner_mean = jnp.mean(values * scaled, axis=-1, keepdims=True)
    grad_values = scale * scaled - values * scale * scale * scale * inner_mean
    grad_gain = jnp.sum(values * scale * grad_out, axis=0)
    return (grad_values, grad_gain)


def swap(block, axis, mask):
    return lax.ppermute(block, axis, [(i, i ^ mask) for i in range(lax.axis_size(axis))])


def after(value, *earlier):
    return lax.optimization_barrier((value,) + earlier)[0]


def tp_sum(block):
    return block + swap(block, "tp", 1)


def to_partner(block, bit):
    return swap(block, "seq", 1 << bit)


def seq_bits():
    return lax.axis_size("seq").bit_length() - 1


def group_size():
    return lax.axis_size("seq") // QUAD


def group_trade(blocks):
    members = [[low + QUAD * high for high in range(group_size())] for low in range(QUAD)]
    return lax.all_to_all(blocks, "seq", 0, 0, axis_index_groups=members, tiled=True)


def add_kernel(index_ref, *refs):
    total = refs[0][...] + refs[1][...]
    refs[2][...] = total.reshape(refs[2].shape)


def add_side(near, got, side):
    unused, groups, rows, cols = near.shape
    index = jnp.zeros((1,), jnp.int32)
    block = pl.BlockSpec((1, 1, rows, cols), lambda i, ref: (side, i, 0, 0))
    return pl.pallas_call(
        add_kernel,
        grid_spec=pltpu.PrefetchScalarGridSpec(
            num_scalar_prefetch=1,
            grid=(groups,),
            in_specs=[block, block],
            out_specs=pl.BlockSpec((1, rows, cols), lambda i, ref: (i, 0, 0)),
        ),
        out_shape=jax.ShapeDtypeStruct((groups, rows, cols), jnp.float32),
        compiler_params=ROOMY,
        cost_estimate=NO_COST,
    )(index, near, got)


def near_kernel(index_ref, *refs):
    out_ref = refs[-1]
    at = 0
    for near_ref, got_ref, crossed_ref in zip(refs[0:-1:3], refs[1:-1:3], refs[2:-1:3]):
        cols = near_ref.shape[3]
        total = near_ref[0, 0] + got_ref[0, 0] + crossed_ref[0]
        out_ref[0, :, at : at + cols] = total
        at += cols


def near_sums(terms, high):
    unused, groups, rows, unused_cols = terms[0][0].shape
    cols = [term[0].shape[3] for term in terms]
    specs, operands = [], []
    for (near, got, crossed), count in zip(terms, cols):
        four = pl.BlockSpec((1, 1, rows, count), lambda i, ref: (0, ref[0] ^ i, 0, 0))
        three = pl.BlockSpec((1, rows, count), lambda i, ref: (ref[0] ^ i, 0, 0))
        specs += [four, four, three]
        operands += [near, got, crossed]
    return pl.pallas_call(
        near_kernel,
        grid_spec=pltpu.PrefetchScalarGridSpec(
            num_scalar_prefetch=1,
            grid=(groups,),
            in_specs=specs,
            out_specs=pl.BlockSpec((1, rows, sum(cols)), lambda i, ref: (i, 0, 0)),
        ),
        out_shape=jax.ShapeDtypeStruct((groups, rows, sum(cols)), jnp.float32),
        compiler_params=ROOMY,
        cost_estimate=NO_COST,
    )(high, *operands)


def grad_blocks_kernel(pairs, first, relative, rows, member_ref, *refs):
    lefts, rights = refs[: len(pairs)], refs[len(pairs) : 2 * len(pairs)]
    far_ref, near_ref = refs[2 * len(pairs) :]
    other = 1 - first
    at = 0
    for left_ref, right_ref, (low, high) in zip(lefts, rights, pairs):
        got = dot_left(left_ref[...], right_ref[:, low:high].astype(jnp.bfloat16))
        places = slice(at, at + high - low)
        for block in range(got.shape[0] // rows):
            place, member = block // QUAD, block % QUAD
            part = got[block * rows : (block + 1) * rows]
            apart = member_ref[0] ^ member
            is_far = apart >> first & 1
            if relative:
                side = apart >> other & 1
            else:
                side = member >> other & 1

            @pl.when(is_far == 1)
            def _():
                if relative:
                    far_ref[side, place, :, places] = part
                else:
                    far_ref[place, side, :, places] = part

            @pl.when(is_far == 0)
            def _():
                if relative:
                    near_ref[side, place, :, places] = part
                else:
                    near_ref[place, side, :, places] = part

        at += high - low


def grad_blocks(terms, first, relative):
    parts = lax.axis_size("seq")
    groups = parts // QUAD
    model_width = terms[0][0].shape[1]
    rows = model_width // parts
    cols = max(128, QUAD * rows)
    places = cols // (QUAD * rows)
    pairs = [(low, high) for unused, unused_right, low, high in terms]
    total = sum(high - low for low, high in pairs)
    member = (lax.axis_index("seq") % QUAD).astype(jnp.int32).reshape(1)
    if relative:
        shape, block = (2, groups, rows, total), (2, places, rows, total)
        out_spec = pl.BlockSpec(block, lambda i, ref: (0, i, 0, 0))
    else:
        shape, block = (groups, 2, rows, total), (places, 2, rows, total)
        out_spec = pl.BlockSpec(block, lambda i, ref: (i, 0, 0, 0))
    out = jax.ShapeDtypeStruct(shape, jnp.float32)
    return pl.pallas_call(
        partial(grad_blocks_kernel, pairs, first, relative, rows),
        grid_spec=pltpu.PrefetchScalarGridSpec(
            num_scalar_prefetch=1,
            grid=(model_width // cols,),
            in_specs=[
                pl.BlockSpec((term[0].shape[0], cols), lambda i, ref: (0, i)) for term in terms
            ]
            + [pl.BlockSpec(term[1].shape, lambda i, ref: (0, 0)) for term in terms],
            out_specs=[out_spec, out_spec],
        ),
        out_shape=[out, out],
        compiler_params=ROOMY,
        cost_estimate=NO_COST,
    )(member, *[term[0] for term in terms], *[term[1] for term in terms])


def segment_ids(lengths, place_count):
    ends = jnp.cumsum(lengths // 8, dtype=jnp.int32)
    places = jnp.arange(place_count, dtype=jnp.int32)
    short_ids = jnp.sum(
        (places[:, None] >= ends[None, :]).astype(jnp.int32), axis=1, dtype=jnp.int32
    )
    return jnp.stack([jnp.zeros_like(short_ids), short_ids])


def scan_heads(seg_now, head_size, xbc, dt_raw, conv_weight, conv_bias, dt_shift, a_logs, skips):
    place_count = xbc.shape[0]
    conv_sum = conv_bias + conv_weight[3] * xbc
    for offset in range(3):
        distance = 3 - offset
        earlier = jnp.pad(xbc, ((distance, 0), (0, 0)))[:place_count]
        seg_earlier = jnp.pad(seg_now, (distance, 0), constant_values=-1)[:place_count]
        same_doc = (seg_earlier == seg_now).astype(jnp.float32)
        conv_sum = conv_sum + conv_weight[offset] * earlier * same_doc[:, None]
    active = jax.nn.silu(conv_sum)
    head_count = dt_raw.shape[1]
    inner = head_count * head_size
    values = active[:, :inner].reshape(place_count, head_count, head_size)
    in_keys = active[:, inner : inner + NS]
    out_keys = active[:, inner + NS :]
    step_sizes = jax.nn.softplus(dt_raw + dt_shift)
    decay_rates = -step_sizes * jnp.exp(a_logs)
    chunk = min(place_count, 512)
    triangle = jnp.tril(jnp.ones((chunk, chunk), jnp.float32))
    state = jnp.zeros((head_count, head_size, NS), jnp.float32)
    seg_last = jnp.int32(-1)
    outputs = []
    for start in range(0, place_count, chunk):
        stop = start + chunk
        x, b, c = values[start:stop], in_keys[start:stop], out_keys[start:stop]
        dt, seg = step_sizes[start:stop], seg_now[start:stop]
        cumulative = jnp.dot(triangle, decay_rates[start:stop], precision=highest)
        allowed = (triangle > 0.0) & (seg[:, None] == seg[None, :])
        ordered = cumulative.T
        gaps = ordered[:, :, None] - ordered[:, None, :]
        decays = jnp.where(allowed, jnp.exp(jnp.where(allowed, gaps, 0.0)), 0.0)
        crossing = jnp.einsum("pn,jn->pj", c, b, precision=highest)
        mixing = crossing[None] * decays * dt.T[:, None, :]
        result = jnp.einsum("hpj,jhd->phd", mixing, x, precision=highest)
        if start > 0:
            entering = jnp.exp(cumulative) * (seg == seg_last).astype(jnp.float32)[:, None]
            result = result + entering[..., None] * jnp.einsum(
                "pn,hdn->phd", c, state, precision=highest
            )
        if stop < place_count:
            last_same = (seg == seg[-1]).astype(jnp.float32)[:, None]
            weight = jnp.exp(cumulative[-1:] - cumulative) * last_same * dt
            through = jnp.exp(cumulative[-1]) * (seg[-1] == seg_last).astype(jnp.float32)
            state = through[:, None, None] * state + jnp.einsum(
                "jh,jhd,jn->hdn", weight, x, b, precision=highest
            )
            seg_last = seg[-1]
        outputs.append(result + skips[:, None] * x)
    return jnp.concatenate(outputs, axis=0).reshape(place_count, inner)


def gated_unit(result, gate_in):
    gated = result * jax.nn.silu(gate_in)
    return gated * rms_scale(gated)


def patch_far_kernel(grad_ref, gain_ref, bytes_ref, out_ref):
    half = grad_ref.shape[1] // 2
    grad_low = grad_ref[:, half:].astype(jnp.bfloat16)
    out_ref[:half] = dot_left(grad_low, bytes_ref[...].astype(jnp.bfloat16))
    out_ref[half:] = jnp.zeros((out_ref.shape[0] - half, out_ref.shape[1]), jnp.float32)

    @pl.when(pl.program_id(0) == 0)
    def _():
        out_ref[half:, : 2 * half] = gain_ref[...]


def patch_far_grad(grad_rows, gain_part, bytes_all):
    places, cols = grad_rows.shape
    total = bytes_all.shape[1]
    rows = cols // 2 + gain_part.shape[0]
    block = 1024
    return pl.pallas_call(
        patch_far_kernel,
        grid=(total // block,),
        in_specs=[
            pl.BlockSpec((places, cols), lambda i: (0, 0)),
            pl.BlockSpec(gain_part.shape, lambda i: (0, 0)),
            pl.BlockSpec((places, block), lambda i: (0, i)),
        ],
        out_specs=pl.BlockSpec((rows, block), lambda i: (0, i)),
        out_shape=jax.ShapeDtypeStruct((rows, total), jnp.float32),
        compiler_params=ROOMY,
        cost_estimate=NO_COST,
    )(grad_rows, gain_part, bytes_all)


def patch_grad_kernel(grad_ref, *refs):
    byte_refs, got_refs, out_ref, order_ref = refs[:8], refs[8:16], refs[16], refs[17]
    width = byte_refs[0].shape[1]

    @pl.when(pl.program_id(0) == 0)
    def _():
        order_ref[...] = feature_order(width)

    grad_low = grad_ref[:, : grad_ref.shape[1] // 2].astype(jnp.bfloat16)
    wide = jnp.concatenate([ref[...].astype(jnp.bfloat16) for ref in byte_refs], axis=1)
    rows = grad_low.shape[1]
    grad = dot_left(grad_low, wide)
    grad = grad + jnp.concatenate([ref[:rows] for ref in got_refs], axis=1)
    high = grad.astype(jnp.bfloat16)
    rest = grad - high.astype(jnp.float32)
    mid = rest.astype(jnp.bfloat16)
    low = (rest - mid.astype(jnp.float32)).astype(jnp.bfloat16)
    order = order_ref[...]
    out_ref[...] = dot_plain(high, order) + (dot_plain(mid, order) + dot_plain(low, order))


def patch_grad(grad_rows, got, bytes_all):
    places, cols = grad_rows.shape
    feature = bytes_all.shape[1] // 8
    chunk = 128
    steps = feature // chunk

    def byte_specs(rows):
        return [
            pl.BlockSpec((rows, chunk), partial(lambda j, i: (0, j * steps + i), j))
            for j in range(8)
        ]

    return pl.pallas_call(
        patch_grad_kernel,
        grid=(steps,),
        in_specs=[pl.BlockSpec((places, cols), lambda i: (0, 0))]
        + byte_specs(places)
        + byte_specs(got.shape[0]),
        out_specs=pl.BlockSpec((cols // 2, 8 * chunk), lambda i: (0, i)),
        out_shape=jax.ShapeDtypeStruct((cols // 2, 8 * feature), jnp.float32),
        scratch_shapes=[pltpu.VMEM((8 * chunk, 8 * chunk), jnp.bfloat16)],
        compiler_params=ROOMY,
        cost_estimate=NO_COST,
    )(grad_rows, *([bytes_all] * 8), *([got] * 8))


def trade(blocks):
    return lax.all_to_all(blocks, "seq", 0, 0, tiled=True)


def grid_iota(shape, axis):
    return lax.broadcasted_iota(jnp.int32, shape, axis)


def dot_fine(left_side, right_side, left_axis, right_axis):
    return lax.dot_general(
        left_side,
        right_side,
        (((left_axis,), (right_axis,)), ((), ())),
        preferred_element_type=jnp.float32,
        precision=highest,
    )


def shifted_down(block, distance):
    rows = grid_iota(block.shape, 0)
    return jnp.where(rows >= distance, pltpu.roll(block, distance, 0), 0.0)


def shifted_up(block, distance):
    count = block.shape[0]
    rows = grid_iota(block.shape, 0)
    return jnp.where(rows < count - distance, pltpu.roll(block, count - distance, 0), 0.0)


def scan_terms(taken_ref, same_ref, conv_ref, head_ref):
    places = taken_ref.shape[0]
    channels = conv_ref.shape[1]
    xbc = taken_ref[:, :channels]
    conv_sum = conv_ref[4:5] + conv_ref[3:4] * xbc
    for k in range(3):
        earlier = shifted_down(xbc, 3 - k) * same_ref[:, k : k + 1]
        conv_sum = conv_sum + conv_ref[k : k + 1] * earlier
    gate = jax.nn.sigmoid(conv_sum)
    active = conv_sum * gate
    raw = taken_ref[:, channels:] + head_ref[0:1]
    steps = jnp.maximum(raw, 0.0) + jnp.log1p(jnp.exp(-jnp.abs(raw)))
    rates = -steps * jnp.exp(head_ref[1:2])
    square = (places, places)
    triangle = jnp.where(grid_iota(square, 0) >= grid_iota(square, 1), 1.0, 0.0)
    running = dot_fine(triangle, rates, 1, 0)
    return xbc, conv_sum, gate, active, raw, steps, rates, triangle, running


def scan_forward_kernel(taken_ref, same_ref, conv_ref, head_ref, seg_col, seg_row, out_ref):
    places, width = out_ref.shape
    terms = scan_terms(taken_ref, same_ref, conv_ref, head_ref)
    active, steps, running = terms[3], terms[5], terms[8]
    values = active[:, :width]
    keys, reads = active[:, width : width + NS], active[:, width + NS :]
    steps_row, running_row = steps.T, running.T
    heads = width // 64
    rows = 128
    for first in range(0, places, rows):
        last = first + rows
        shape = (rows, last)
        allowed = (seg_col[first:last] == seg_row[:, :last]) & (
            grid_iota(shape, 0) + first >= grid_iota(shape, 1)
        )
        crossing = dot_fine(reads[first:last], keys[:last], 1, 1)
        lane = grid_iota((rows, width), 1) // 64
        total = head_ref[2:3] * values[first:last]
        for h in range(heads):
            gaps = running[first:last, h : h + 1] - running_row[h : h + 1, :last]
            decays = jnp.exp(jnp.where(allowed, gaps, masked_score))
            mixing = crossing * decays * steps_row[h : h + 1, :last]
            part = dot_fine(mixing, values[:last], 1, 0)
            total = total + jnp.where(lane == h, part, 0.0)
        out_ref[first:last] = total


def scan_backward_kernel(
    taken_ref,
    same_ref,
    conv_ref,
    head_ref,
    seg_col,
    seg_row,
    grad_ref,
    out_ref,
    conv_grad_ref,
    head_grad_ref,
    values_grad,
    keys_grad,
    reads_grad,
    rows_grad,
    cols_grad,
):
    places, width = values_grad.shape
    terms = scan_terms(taken_ref, same_ref, conv_ref, head_ref)
    xbc, conv_sum, gate, active, raw, steps, rates, triangle, running = terms
    channels = xbc.shape[1]
    values = active[:, :width]
    keys, reads = active[:, width : width + NS], active[:, width + NS :]
    steps_row, running_row = steps.T, running.T
    heads = width // 64
    rows = 128
    grad = grad_ref[...]
    values_grad[...] = head_ref[2:3] * grad
    keys_grad[...] = jnp.zeros_like(keys_grad)
    rows_grad[...] = jnp.zeros_like(rows_grad)
    cols_grad[...] = jnp.zeros_like(cols_grad)
    for first in range(0, places, rows):
        last = first + rows
        shape = (rows, last)
        allowed = (seg_col[first:last] == seg_row[:, :last]) & (
            grid_iota(shape, 0) + first >= grid_iota(shape, 1)
        )
        crossing = dot_fine(reads[first:last], keys[:last], 1, 1)
        crossing_grad = jnp.zeros(shape, jnp.float32)
        grad_rows = grad[first:last]
        lane = grid_iota((rows, width), 1) // 64
        wide_lane = grid_iota((last, width), 1) // 64
        column = grid_iota((rows, 128), 1)
        down = jnp.zeros((rows, 128), jnp.float32)
        for h in range(heads):
            gaps = running[first:last, h : h + 1] - running_row[h : h + 1, :last]
            decays = jnp.exp(jnp.where(allowed, gaps, masked_score))
            step_row = steps_row[h : h + 1, :last]
            weighted = decays * step_row
            mixing = crossing * weighted
            own_grad = jnp.where(lane == h, grad_rows, 0.0)
            mixing_grad = dot_fine(own_grad, values[:last], 1, 1)
            back = dot_fine(mixing, own_grad, 0, 0)
            values_grad[:last] += jnp.where(wide_lane == h, back, 0.0)
            crossing_grad = crossing_grad + mixing_grad * weighted
            step_part = jnp.sum(mixing_grad * crossing * decays, axis=0, keepdims=True)
            gap_part = mixing_grad * mixing
            down = jnp.where(column == h, jnp.sum(gap_part, axis=1, keepdims=True), down)
            cols_grad[h : h + 1, :last] += step_part
            cols_grad[heads + h : heads + h + 1, :last] += step_part * step_row
        rows_grad[first:last] += down
        reads_grad[first:last] = dot_fine(crossing_grad, keys[:last], 1, 0)
        keys_grad[:last] += dot_fine(crossing_grad, reads[first:last], 0, 0)
    turned = cols_grad[...].T
    column = grid_iota(turned.shape, 1)
    step_grad = jnp.where(column < heads, turned, 0.0)
    ended = pltpu.roll(turned, turned.shape[1] - heads, 1)
    running_grad = jnp.where(column < heads, rows_grad[...] - ended, 0.0)
    rates_grad = dot_fine(triangle, running_grad, 0, 0)
    step_grad = step_grad - rates_grad * jnp.exp(head_ref[1:2])
    raw_grad = step_grad * jax.nn.sigmoid(raw)
    out_ref[:, channels:] = raw_grad
    lane = grid_iota((places, width), 1) // 64
    product = jnp.sum(grad * values, axis=0, keepdims=True)
    head_grad_ref[...] = jnp.zeros_like(head_grad_ref)
    head_grad_ref[0:1] = jnp.sum(raw_grad, axis=0, keepdims=True)
    head_grad_ref[1:2] = jnp.sum(rates_grad * rates, axis=0, keepdims=True)
    skip_lane = grid_iota((1, width), 1)
    skip_grad = jnp.zeros((1, width), jnp.float32)
    for h in range(heads):
        own = jnp.sum(jnp.where(skip_lane // 64 == h, product, 0.0), axis=1, keepdims=True)
        skip_grad = jnp.where(skip_lane == h, own, skip_grad)
    head_grad_ref[2:3] = skip_grad
    active_grad = jnp.concatenate([values_grad[...], keys_grad[...], reads_grad[...]], axis=1)
    conv_grad = active_grad * gate * (1.0 + conv_sum * (1.0 - gate))
    back = conv_ref[3:4] * conv_grad
    conv_grad_ref[...] = jnp.zeros_like(conv_grad_ref)
    conv_grad_ref[3:4] = jnp.sum(conv_grad * xbc, axis=0, keepdims=True)
    conv_grad_ref[4:5] = jnp.sum(conv_grad, axis=0, keepdims=True)
    for k in range(3):
        kept = conv_grad * same_ref[:, k : k + 1]
        back = back + conv_ref[k : k + 1] * shifted_up(kept, 3 - k)
        conv_grad_ref[k : k + 1] = jnp.sum(
            kept * shifted_down(xbc, 3 - k), axis=0, keepdims=True
        )
    out_ref[:, :channels] = back


def scan_forward(args, width):
    places = args[0].shape[0]
    return pl.pallas_call(
        scan_forward_kernel,
        out_shape=jax.ShapeDtypeStruct((places, width), jnp.float32),
        compiler_params=ROOMY,
        cost_estimate=NO_COST,
    )(*args)


def scan_backward(args, grad):
    places, width = grad.shape
    channels = args[2].shape[1]
    f32 = jnp.float32
    return pl.pallas_call(
        scan_backward_kernel,
        out_shape=[
            jax.ShapeDtypeStruct((places, channels + 128), f32),
            jax.ShapeDtypeStruct((8, channels), f32),
            jax.ShapeDtypeStruct((8, 128), f32),
        ],
        scratch_shapes=[
            pltpu.VMEM((places, width), f32),
            pltpu.VMEM((places, NS), f32),
            pltpu.VMEM((places, NS), f32),
            pltpu.VMEM((places, 128), f32),
            pltpu.VMEM((128, places), f32),
        ],
        compiler_params=ROOMY,
        cost_estimate=NO_COST,
    )(*args, grad)


def patch_lanes(block):
    shape = (block // 8, 8, block)
    return grid_iota(shape, 0) == grid_iota(shape, 2) // 8


def folded(scores, same_patch):
    split = scores.reshape(same_patch.shape)
    return jnp.sum(jnp.where(same_patch, split, 0.0), axis=0)


def unfolded(rows, same_patch):
    spread = jnp.where(same_patch, rows[None], 0.0)
    return spread.reshape(-1, rows.shape[1]).astype(jnp.bfloat16)


def softmax_rows(scores, causal):
    scores = jnp.where(causal, scores, masked_score)
    top = jnp.max(scores, axis=1, keepdims=True)
    powers = jnp.exp(scores - top)
    return powers / jnp.sum(powers, axis=1, keepdims=True)


def head_places(rows, head_cols, block):
    return [
        (slice(first, first + block), [j * head_cols + pair * 128 for j in range(3)])
        for first in range(0, rows, block)
        for pair in range(head_cols // 128)
    ]


def all_scores(qkv_ref, places, lane, same_patch):
    scores = []
    for rows, (query, key, unused) in places:
        queries = qkv_ref[rows, query : query + 128] * 0.125
        keys = qkv_ref[rows, key : key + 128]
        for h in range(2):
            own = jnp.where(lane == h, queries, 0)
            scores.append(folded(dot_trans(keys, own), same_patch))
    return jnp.stack(scores)


def attn_forward_kernel(
    bytes_ref, patch_ref, gain_ref, qkv_w_ref, o_w_ref, x_ref, a_ref, qkv_ref, o_ref, out_ref
):
    rows = bytes_ref.shape[0]
    spread = jnp.broadcast_to(patch_ref[...][:, None], (rows // 8, 8, patch_ref.shape[1]))
    x = bytes_ref[...].astype(jnp.float32) + spread.reshape(bytes_ref.shape)
    x_ref[...] = x
    attn_in = (x * rms_scale(x) * gain_ref[...]).astype(jnp.bfloat16)
    a_ref[...] = attn_in
    qkv_ref[...] = dot_plain(attn_in, qkv_w_ref[...]).astype(jnp.bfloat16)
    head_cols = o_ref.shape[1]
    block = 128
    same_patch = patch_lanes(block)
    causal = grid_iota((8, block), 0) <= grid_iota((8, block), 1) % 8
    lane = grid_iota((block, 128), 1) // AD
    places = head_places(rows, head_cols, block)
    probs = softmax_rows(all_scores(qkv_ref, places, lane, same_patch), causal)
    for at, (row_place, (query, unused, value)) in enumerate(places):
        values = qkv_ref[row_place, value : value + 128]
        parts = [dot_left(unfolded(probs[2 * at + h], same_patch), values) for h in range(2)]
        total = jnp.where(lane == 0, parts[0], parts[1])
        o_ref[row_place, query : query + 128] = total.astype(jnp.bfloat16)
    out_ref[...] = dot_trans(o_ref[...], o_w_ref[...])


def attn_forward(bytes_rows, patch_rows, gain, w_qkv, w_o):
    rows, width = bytes_rows.shape
    block = 256
    cols, head_cols = w_qkv.shape[1], w_o.shape[1]
    f32, bf16 = jnp.float32, jnp.bfloat16

    def by_rows(cols):
        return pl.BlockSpec((block, cols), lambda i: (i, 0))

    def whole(shape):
        return pl.BlockSpec(shape, lambda i: (0, 0))

    return pl.pallas_call(
        attn_forward_kernel,
        grid=(rows // block,),
        in_specs=[
            by_rows(width),
            pl.BlockSpec((block // 8, width), lambda i: (i, 0)),
            whole((1, width)),
            whole(w_qkv.shape),
            whole(w_o.shape),
        ],
        out_specs=[by_rows(width), by_rows(width), by_rows(cols), by_rows(head_cols), by_rows(width)],
        out_shape=[
            jax.ShapeDtypeStruct((rows, width), f32),
            jax.ShapeDtypeStruct((rows, width), bf16),
            jax.ShapeDtypeStruct((rows, cols), bf16),
            jax.ShapeDtypeStruct((rows, head_cols), bf16),
            jax.ShapeDtypeStruct((rows, width), f32),
        ],
        compiler_params=ROOMY,
        cost_estimate=NO_COST,
    )(bytes_rows, patch_rows, gain.reshape(1, width), w_qkv, w_o)


def attn_backward_kernel(
    x_ref,
    final_ref,
    own_ref,
    other_ref,
    gain_ref,
    qkv_ref,
    qkv_w_ref,
    o_w_ref,
    mid_ref,
    low_ref,
    qkv_grad_ref,
    out_ref,
    gain_grad_ref,
):
    rows = x_ref.shape[0]
    back, gain_grad = rms_back(x_ref[...], gain_ref[...], own_ref[...] + other_ref[...])
    mid = final_ref[...] + back
    mid_ref[...] = mid
    low_ref[...] = mid.astype(jnp.bfloat16)
    gain_grad = gain_grad.reshape(1, -1)

    @pl.when(pl.program_id(0) == 0)
    def _():
        gain_grad_ref[...] = gain_grad

    @pl.when(pl.program_id(0) > 0)
    def _():
        gain_grad_ref[...] += gain_grad

    mixed_grad = dot_plain(low_ref[...], o_w_ref[...]).astype(jnp.bfloat16)
    head_cols = mixed_grad.shape[1]
    block = 128
    same_patch = patch_lanes(block)
    causal = grid_iota((8, block), 0) <= grid_iota((8, block), 1) % 8
    lane = grid_iota((block, 128), 1) // AD
    places = head_places(rows, head_cols, block)
    probs = softmax_rows(all_scores(qkv_ref, places, lane, same_patch), causal)
    probs_grads = []
    for row_place, (query, unused, value) in places:
        values = qkv_ref[row_place, value : value + 128]
        out_grad = mixed_grad[row_place, query : query + 128]
        for h in range(2):
            own_grad = jnp.where(lane == h, out_grad, 0)
            probs_grads.append(folded(dot_trans(values, own_grad), same_patch))
    probs_grad = jnp.stack(probs_grads)
    inner = jnp.sum(probs * probs_grad, axis=1, keepdims=True)
    scores_grad = probs * (probs_grad - inner)
    for at, (row_place, cols) in enumerate(places):
        query, key, unused = cols
        queries = qkv_ref[row_place, query : query + 128]
        keys = qkv_ref[row_place, key : key + 128]
        out_grad = mixed_grad[row_place, query : query + 128]
        parts = []
        for h in range(2):
            own_scores = unfolded(scores_grad[2 * at + h], same_patch)
            parts.append(
                (
                    dot_left(own_scores, keys) * 0.125,
                    dot_plain(own_scores, queries) * 0.125,
                    dot_plain(unfolded(probs[2 * at + h], same_patch), out_grad),
                )
            )
        for j in range(3):
            grad = jnp.where(lane == 0, parts[0][j], parts[1][j])
            qkv_grad_ref[row_place, cols[j] : cols[j] + 128] = grad.astype(jnp.bfloat16)
    out_ref[...] = dot_trans(qkv_grad_ref[...], qkv_w_ref[...])


def attn_backward(x_rows, final_grad, own_part, other_part, gain, qkv, w_qkv, w_o):
    rows, width = x_rows.shape
    block = 256
    cols = w_qkv.shape[1]
    f32, bf16 = jnp.float32, jnp.bfloat16

    def by_rows(cols):
        return pl.BlockSpec((block, cols), lambda i: (i, 0))

    def whole(shape):
        return pl.BlockSpec(shape, lambda i: (0, 0))

    return pl.pallas_call(
        attn_backward_kernel,
        grid=(rows // block,),
        in_specs=[by_rows(width)] * 4
        + [whole((1, width)), by_rows(cols), whole(w_qkv.shape), whole(w_o.shape)],
        out_specs=[
            by_rows(width),
            by_rows(width),
            by_rows(cols),
            by_rows(width),
            whole((1, width)),
        ],
        out_shape=[
            jax.ShapeDtypeStruct((rows, width), f32),
            jax.ShapeDtypeStruct((rows, width), bf16),
            jax.ShapeDtypeStruct((rows, cols), bf16),
            jax.ShapeDtypeStruct((rows, width), f32),
            jax.ShapeDtypeStruct((1, width), f32),
        ],
        compiler_params=ROOMY,
        cost_estimate=NO_COST,
    )(x_rows, final_grad, own_part, other_part, gain.reshape(1, width), qkv, w_qkv, w_o)


def mlp_in_kernel(core_ref, x_ref, own_ref, other_ref, gain_ref, out_ref, low_ref, half_ref):
    x = x_ref[...] + (own_ref[...] + other_ref[...])
    out_ref[...] = x
    unit = x * rms_scale(x)
    low_ref[...] = (unit * gain_ref[...]).astype(jnp.bfloat16)
    width = half_ref.shape[1]
    half_ref[...] = jnp.where(core_ref[0] == 0, unit[:, :width], unit[:, width:])


def mlp_in(x_rows, own_part, other_part, gain):
    rows, width = x_rows.shape
    block = 128
    core = lax.axis_index("tp").astype(jnp.int32).reshape(1)

    def by_rows(cols):
        return pl.BlockSpec((block, cols), lambda i, ref: (i, 0))

    return pl.pallas_call(
        mlp_in_kernel,
        grid_spec=pltpu.PrefetchScalarGridSpec(
            num_scalar_prefetch=1,
            grid=(rows // block,),
            in_specs=[by_rows(width)] * 3 + [pl.BlockSpec((1, width), lambda i, ref: (0, 0))],
            out_specs=[by_rows(width), by_rows(width), by_rows(width // 2)],
        ),
        out_shape=[
            jax.ShapeDtypeStruct((rows, width), jnp.float32),
            jax.ShapeDtypeStruct((rows, width), jnp.bfloat16),
            jax.ShapeDtypeStruct((rows, width // 2), jnp.float32),
        ],
        compiler_params=ROOMY,
        cost_estimate=NO_COST,
    )(core, x_rows, own_part, other_part, gain.reshape(1, width))


def units_in_halves(
    mlp_low, grad_ref, gate_w_ref, up_w_ref, hidden_ref, gate_ref, up_ref
):
    half = grad_ref.shape[1] // 2
    for at in range(2):
        cols = slice(at * half, (at + 1) * half)
        hidden, gate, up = hidden_parts(
            mlp_low, grad_ref[:, cols], gate_w_ref[:, cols], up_w_ref[:, cols]
        )
        hidden_ref[:, cols] = hidden
        gate_ref[:, cols] = gate
        up_ref[:, cols] = up


def mlp_kernel(
    in_ref, grad_ref, gate_w_ref, up_w_ref, hidden_ref, gate_ref, up_ref, out_ref, total_ref
):
    mlp_low = in_ref[...]
    units_in_halves(
        mlp_low, grad_ref, gate_w_ref, up_w_ref, hidden_ref, gate_ref, up_ref
    )
    part = dot_trans(gate_ref[...], gate_w_ref[...]) + dot_trans(up_ref[...], up_w_ref[...])
    step = pl.program_id(0)

    @pl.when(step == 0)
    def _():
        total_ref[...] = part

    @pl.when(step > 0)
    def _():
        total_ref[...] += part

    @pl.when(step == pl.num_programs(0) - 1)
    def _():
        out_ref[...] = total_ref[...]


def mlp_rows(mlp_low, grad_hidden, w_gate, w_up):
    rows, width = mlp_low.shape
    units = w_gate.shape[1]
    block = 512
    by_units = pl.BlockSpec((rows, block), lambda i: (0, i))
    by_weights = pl.BlockSpec((width, block), lambda i: (0, i))
    whole = pl.BlockSpec((rows, width), lambda i: (0, 0))
    low = jax.ShapeDtypeStruct((rows, units), jnp.bfloat16)
    return pl.pallas_call(
        mlp_kernel,
        grid=(units // block,),
        in_specs=[whole, by_units, by_weights, by_weights],
        out_specs=[by_units, by_units, by_units, whole],
        out_shape=[low, low, low, jax.ShapeDtypeStruct((rows, width), jnp.float32)],
        scratch_shapes=[pltpu.VMEM((rows, width), jnp.float32)],
        compiler_params=ROOMY,
        cost_estimate=NO_COST,
    )(mlp_low, grad_hidden, w_gate, w_up)


def feature_order(width):
    shape = (8 * width, 8 * width)
    row, col = grid_iota(shape, 0), grid_iota(shape, 1)
    return jnp.where(row == (col % 8) * width + col // 8, 1.0, 0.0).astype(jnp.bfloat16)


def patch_in_kernel(core_ref, bytes_ref, weight_ref, wide_ref, out_ref, rows_ref, order_ref):
    places, feature = wide_ref.shape[0], wide_ref.shape[1] // 8
    chunk = weight_ref.shape[1] // 8
    step = pl.program_id(0)

    @pl.when(step == 0)
    def _():
        order_ref[...] = feature_order(chunk)
        for at in range(feature // 128):
            low = at * 128
            rows_ref[at] = bytes_ref[:, low : low + 128].astype(jnp.float32)
            for j in range(8):
                wide_ref[:, j * feature + low : j * feature + low + 128] = rows_ref[
                    at, pl.ds(j, places, stride=8), :
                ]

    parts = [
        wide_ref[:, pl.ds(pl.multiple_of(j * feature + step * chunk, 128), chunk)]
        for j in range(8)
    ]
    by_byte = jnp.concatenate(parts, axis=1).astype(jnp.bfloat16)
    by_feature = dot_plain(by_byte, order_ref[...]).astype(jnp.bfloat16)
    part = dot_trans(by_feature, weight_ref[...])

    @pl.when(step == 0)
    def _():
        out_ref[...] = part

    @pl.when(step > 0)
    def _():
        out_ref[...] += part


def patch_in(byte_rows, w_patch):
    rows, model_width = byte_rows.shape
    out_width, cols = w_patch.shape
    feature, chunk = cols // 8, 128
    core = lax.axis_index("tp").astype(jnp.int32).reshape(1)
    f32 = jnp.float32
    return pl.pallas_call(
        patch_in_kernel,
        grid_spec=pltpu.PrefetchScalarGridSpec(
            num_scalar_prefetch=1,
            grid=(feature // chunk,),
            in_specs=[
                pl.BlockSpec((rows, feature), lambda i, ref: (0, ref[0])),
                pl.BlockSpec((out_width, 8 * chunk), lambda i, ref: (0, i)),
            ],
            out_specs=[
                pl.BlockSpec((rows // 8, cols), lambda i, ref: (0, 0)),
                pl.BlockSpec((rows // 8, out_width), lambda i, ref: (0, 0)),
            ],
            scratch_shapes=[
                pltpu.VMEM((feature // 128, rows, 128), f32),
                pltpu.VMEM((8 * chunk, 8 * chunk), jnp.bfloat16),
            ],
        ),
        out_shape=[
            jax.ShapeDtypeStruct((rows // 8, cols), f32),
            jax.ShapeDtypeStruct((rows // 8, out_width), f32),
        ],
        compiler_params=ROOMY,
        cost_estimate=NO_COST,
    )(core, byte_rows, w_patch)


def final_kernel(
    member_ref,
    own_ref,
    other_ref,
    mask_ref,
    own_head_ref,
    other_head_ref,
    weight_ref,
    low_ref,
    hidden_ref,
    mine_ref,
    mine_low_ref,
):
    own = (own_ref[...] * mask_ref[...]).astype(jnp.bfloat16)
    other = (other_ref[...] * mask_ref[...]).astype(jnp.bfloat16)
    other_head = other_head_ref[...].astype(jnp.bfloat16)
    total = dot_trans(own, own_head_ref[...]) + dot_trans(other, other_head)
    low = total.astype(jnp.bfloat16)
    low_ref[...] = low
    hidden_ref[...] = dot_plain(low, weight_ref[...])

    @pl.when(pl.program_id(0) == 0)
    def _():
        mine_ref[...] = total
        mine_low_ref[...] = low


def final_grads(own, other, mask, own_head, other_head, w_down, member):
    rows, cols = own.shape
    width = own_head.shape[0]
    block = rows // group_size()
    units = w_down.shape[1] // group_size()
    f32, bf16 = jnp.float32, jnp.bfloat16

    def by_rows(cols):
        return pl.BlockSpec((block, cols), lambda i, ref: (i, 0))

    head = pl.BlockSpec((width, cols), lambda i, ref: (0, 0))
    mine = pl.BlockSpec((block, width), lambda i, ref: (0, 0))
    return pl.pallas_call(
        final_kernel,
        grid_spec=pltpu.PrefetchScalarGridSpec(
            num_scalar_prefetch=1,
            grid=(group_size(),),
            in_specs=[by_rows(cols), by_rows(cols), by_rows(1), head, head]
            + [pl.BlockSpec((width, units), lambda i, ref: (0, ref[0]))],
            out_specs=[by_rows(width), by_rows(units), mine, mine],
        ),
        out_shape=[
            jax.ShapeDtypeStruct((rows, width), bf16),
            jax.ShapeDtypeStruct((rows, units), f32),
            jax.ShapeDtypeStruct((block, width), f32),
            jax.ShapeDtypeStruct((block, width), bf16),
        ],
        compiler_params=ROOMY,
        cost_estimate=NO_COST,
    )(member, own, other, mask, own_head, other_head, w_down)


def group_mlp_kernel(
    place_ref,
    own_ref,
    other_ref,
    gain_ref,
    grad_ref,
    gate_w_ref,
    up_w_ref,
    in_ref,
    hidden_ref,
    gate_ref,
    up_ref,
):
    own, other = own_ref[0], other_ref[0]
    first = place_ref[1] == 0
    halves = [jnp.where(first, own, other), jnp.where(first, other, own)]
    low = (jnp.concatenate(halves, axis=1) * gain_ref[...]).astype(jnp.bfloat16)
    in_ref[...] = low
    units_in_halves(low, grad_ref, gate_w_ref, up_w_ref, hidden_ref, gate_ref, up_ref)


def group_mlp(own_half, other_half, gain, grad_hidden, w_gate, w_up, member):
    rows, half = grad_hidden.shape[0] // group_size(), own_half.shape[2]
    width, units = 2 * half, w_gate.shape[1] // group_size()
    bf16 = jnp.bfloat16
    place = jnp.concatenate([member, lax.axis_index("tp").astype(jnp.int32).reshape(1)])

    def by_rows(cols):
        return pl.BlockSpec((rows, cols), lambda i, ref: (i, 0))

    halves = pl.BlockSpec((1, rows, half), lambda i, ref: (i ^ ref[0], 0, 0))
    weights = pl.BlockSpec((width, units), lambda i, ref: (0, ref[0]))
    low = jax.ShapeDtypeStruct((group_size() * rows, units), bf16)
    return pl.pallas_call(
        group_mlp_kernel,
        grid_spec=pltpu.PrefetchScalarGridSpec(
            num_scalar_prefetch=1,
            grid=(group_size(),),
            in_specs=[
                halves,
                halves,
                pl.BlockSpec((1, width), lambda i, ref: (0, 0)),
                by_rows(units),
                weights,
                weights,
            ],
            out_specs=[by_rows(width), by_rows(units), by_rows(units), by_rows(units)],
        ),
        out_shape=[jax.ShapeDtypeStruct((group_size() * rows, width), bf16), low, low, low],
        compiler_params=ROOMY,
        cost_estimate=NO_COST,
    )(place, own_half, other_half, gain.reshape(1, width), grad_hidden, w_gate, w_up)


def bytes_grad_kernel(core_ref, grad_ref, weight_ref, stream_ref, out_ref, order_ref):
    places = grad_ref.shape[0]
    chunk = weight_ref.shape[1] // 8

    @pl.when(pl.program_id(0) == 0)
    def _():
        order_ref[...] = feature_order(chunk)

    by_feature = dot_plain(grad_ref[...].astype(jnp.bfloat16), weight_ref[...])
    high = by_feature.astype(jnp.bfloat16)
    rest = by_feature - high.astype(jnp.float32)
    mid = rest.astype(jnp.bfloat16)
    low = (rest - mid.astype(jnp.float32)).astype(jnp.bfloat16)
    order = order_ref[...]
    by_byte = dot_trans(high, order) + (dot_trans(mid, order) + dot_trans(low, order))
    for j in range(8):
        rows = pl.ds(j, places, stride=8)
        out_ref[rows, :] = stream_ref[rows, :] + by_byte[:, j * chunk : (j + 1) * chunk]


def bytes_grad(grad_patch, w_patch, grad_stream):
    places, width = grad_patch.shape
    rows = grad_stream.shape[0]
    cols = w_patch.shape[1]
    feature, chunk = cols // 8, 128
    core = lax.axis_index("tp").astype(jnp.int32).reshape(1)
    return pl.pallas_call(
        bytes_grad_kernel,
        grid_spec=pltpu.PrefetchScalarGridSpec(
            num_scalar_prefetch=1,
            grid=(feature // chunk,),
            in_specs=[
                pl.BlockSpec((places, width), lambda i, ref: (0, 0)),
                pl.BlockSpec((width, 8 * chunk), lambda i, ref: (0, i)),
                pl.BlockSpec((rows, chunk), lambda i, ref: (0, ref[0] * (feature // chunk) + i)),
            ],
            out_specs=pl.BlockSpec((rows, chunk), lambda i, ref: (0, i)),
            scratch_shapes=[pltpu.VMEM((8 * chunk, 8 * chunk), jnp.bfloat16)],
        ),
        out_shape=jax.ShapeDtypeStruct((rows, feature), jnp.float32),
        compiler_params=ROOMY,
        cost_estimate=NO_COST,
    )(core, grad_patch, w_patch, grad_stream)


def body(
    byte_states,
    lengths,
    w_patch,
    norm_global,
    w_in,
    conv_w,
    conv_b,
    dt_bias,
    a_log,
    d_skip,
    mix_gain,
    w_out,
    norm_attn,
    w_qkv,
    w_o,
    norm_mlp,
    w_gate,
    w_up,
    w_down,
    w_head,
    d_logits,
):
    streams, local_rows, model_width = byte_states.shape
    patch_count = local_rows // 8
    patch_total = streams * patch_count
    row_total = streams * local_rows
    feature = w_patch.shape[1] // 8
    inner_width = w_out.shape[1]
    channels = conv_w.shape[1]
    head_total = dt_bias.shape[0]
    head_cols = w_head.shape[1]
    parts = lax.axis_size("seq")
    tp_index = lax.axis_index("tp")
    seq_index = lax.axis_index("seq")
    places = parts * patch_count
    f32 = jnp.float32

    lanes = parts // streams
    width = inner_width // lanes
    full_head = inner_width // head_total
    own_heads = max(1, width // full_head)
    shared = max(1, full_head // width)
    head_size = width // own_heads
    own_stream = seq_index // lanes
    first_col = (seq_index % lanes) * width
    first_head = first_col // full_head

    seg_full = segment_ids(lengths, places)
    seg_own = lax.dynamic_slice_in_dim(seg_full, seq_index * patch_count, patch_count, 1)
    seg_stream = lax.dynamic_index_in_dim(seg_full, own_stream, 0, keepdims=False)
    valid = (seg_own < lengths.shape[0]).astype(f32).reshape(patch_total, 1)
    byte_valid = jnp.repeat(valid, 8, axis=0)

    member, members = seq_index // QUAD, group_size()
    raw_logits = d_logits.reshape(row_total, head_cols)
    raw_wide = raw_logits.astype(f32)
    group_valid = []
    for apart in range(members):
        device = seq_index ^ QUAD * apart
        group_seg = lax.dynamic_slice_in_dim(seg_full, device * patch_count, patch_count, 1)
        group_valid.append((group_seg < lengths.shape[0]).astype(f32))
    group_valid = jnp.stack(group_valid).reshape(members, patch_total, 1)
    group_bytes_valid = jnp.repeat(group_valid.reshape(-1, 1), 8, axis=0)
    apart_raw = [swap(raw_wide, "seq", QUAD * apart) for apart in range(1, members)]
    other_head = swap(w_head.astype(f32), "tp", 1)
    place_index = member.astype(jnp.int32).reshape(1)
    bytes_wide, patch_part = patch_in(byte_states.reshape(row_total, model_width), w_patch)
    patch_out = tp_sum(patch_part)
    gain_global = norm_global.astype(f32)
    unit_patch = patch_out * rms_scale(patch_out)
    u_low = (unit_patch * gain_global).astype(jnp.bfloat16)
    half_width = model_width // 2
    proj = dot_plain(u_low, w_in).reshape(streams, patch_count, -1)
    gate_in = proj[..., :inner_width]
    xbc = proj[..., inner_width : inner_width + channels]
    dt_raw = proj[..., inner_width + channels :]

    def by_lane(columns):
        split = columns.reshape(streams, patch_count, lanes, -1)
        return jnp.moveaxis(split, 2, 1).reshape(parts, patch_count, -1)

    def from_lanes(blocks):
        split = blocks.reshape(streams, lanes, patch_count, -1)
        return jnp.moveaxis(split, 1, 2).reshape(streams, patch_count, -1)

    def to_all_lanes(columns):
        wide = jnp.broadcast_to(
            columns[:, None], (streams, lanes, patch_count, columns.shape[-1])
        )
        return wide.reshape(parts, patch_count, -1)

    pad_width = 128 - own_heads
    dt_lanes = by_lane(jnp.repeat(dt_raw, shared, axis=2))
    sent = jnp.concatenate(
        [
            by_lane(xbc[..., :inner_width]),
            to_all_lanes(xbc[..., inner_width:]),
            jnp.pad(dt_lanes, ((0, 0), (0, 0), (0, pad_width))),
        ],
        axis=-1,
    )
    taken = trade(sent)
    row_side = [
        [device for device in range(parts) if (device & 1) == side] for side in range(2)
    ]
    bytes_all = lax.all_gather(
        bytes_wide, "seq", axis=0, axis_index_groups=row_side, tiled=True
    )
    taken = after(taken, bytes_wide).reshape(places, -1)
    scan_width = width + channels - inner_width

    def own_cols(param):
        mine = lax.dynamic_slice_in_dim(param, first_col, width, param.ndim - 1)
        return jnp.concatenate([mine, param[..., inner_width:]], axis=-1).astype(f32)

    def own_head(param):
        return lax.dynamic_slice_in_dim(param, first_head, own_heads, 0).astype(f32)

    use_kernel = places == 512 and width == 128
    if use_kernel:
        padded_seg = jnp.pad(seg_stream, (3, 0), constant_values=-1)
        same = jnp.stack(
            [(padded_seg[k : k + places] == seg_stream).astype(f32) for k in range(3)]
            + [jnp.zeros((places,), f32)] * 5,
            axis=1,
        )
        conv_pack = jnp.concatenate(
            [own_cols(conv_w), own_cols(conv_b)[None], jnp.zeros((3, scan_width), f32)]
        )
        head_pack = jnp.stack(
            [jnp.pad(own_head(dt_bias), (0, 128 - own_heads))]
            + [jnp.pad(own_head(a_log), (0, 128 - own_heads))]
            + [jnp.repeat(own_head(d_skip), head_size)]
            + [jnp.zeros((128,), f32)] * 5
        )
        scan_args = (taken, same, conv_pack, head_pack, seg_stream[:, None], seg_stream[None])
        scanned = scan_forward(scan_args, width)
    else:
        scan_args = (
            taken[:, :scan_width],
            taken[:, scan_width : scan_width + own_heads],
            own_cols(conv_w),
            own_cols(conv_b),
            own_head(dt_bias),
            own_head(a_log),
            own_head(d_skip),
        )
        scanned, scan_back = jax.vjp(partial(scan_heads, seg_stream, head_size), *scan_args)
    result = trade(scanned.reshape(parts, patch_count, width))
    group_raw = jnp.concatenate(
        [raw_wide] + [after(raw, scanned) for raw in apart_raw], axis=0
    )
    other_raw = swap(group_raw, "tp", 1)
    grad_logits = raw_logits * byte_valid.astype(jnp.bfloat16)
    group_final, group_grad_hidden, grad_final, grad_mlp_low = final_grads(
        group_raw,
        other_raw,
        group_bytes_valid,
        w_head,
        other_head,
        w_down,
        place_index,
    )
    grad_hidden = dot_plain(grad_mlp_low, w_down)
    hidden_part = w_gate.shape[1] // members

    result = from_lanes(after(result, group_grad_hidden, grad_hidden))
    unit_normed, norm_back = jax.vjp(gated_unit, result, gate_in)
    mix_scale = mix_gain.astype(f32)
    normed_low = (unit_normed * mix_scale).reshape(patch_total, -1).astype(jnp.bfloat16)


    def quarters(columns):
        split = columns.reshape(patch_total, members, -1)
        return jnp.moveaxis(split, 1, 0)

    def by_apart(blocks):
        return [
            lax.dynamic_index_in_dim(blocks, member ^ apart, 0, keepdims=False)
            for apart in range(members)
        ]

    def group_swap(blocks):
        return [blocks[0]] + [swap(blocks[k], "seq", QUAD * k) for k in range(1, members)]

    def joined(blocks, turn):
        return jnp.concatenate([after(block, turn) for block in blocks], axis=0)

    early_got = group_swap(
        [
            jnp.concatenate([unit_patch, part], axis=-1)
            for part in by_apart(quarters(unit_normed))
        ]
    )
    global_out = patch_out + valid * tp_sum(dot_trans(normed_low, w_out))
    gain_attn = norm_attn.astype(f32)
    gain_mlp = norm_mlp.astype(f32)
    stream_in, attn_in, qkv, mixed_low, attn_part = attn_forward(
        byte_states.reshape(row_total, model_width), global_out, gain_attn, w_qkv, w_o
    )
    after_attn, mlp_low, unit_half = mlp_in(
        stream_in, attn_part, swap(attn_part, "tp", 1), gain_mlp
    )
    hidden_low, grad_gate_low, grad_up_low, grad_mlp_part = mlp_rows(
        after(mlp_low, unit_half), grad_hidden, w_gate, w_up
    )
    group_halves = group_trade(jnp.broadcast_to(unit_half[None], (members,) + unit_half.shape))
    grad_mlp_other = swap(grad_mlp_part, "tp", 1)
    after_mlp = after_attn + tp_sum(dot_trans(after(hidden_low, grad_mlp_part), w_down))
    final_low = after_mlp.astype(jnp.bfloat16)
    logits = dot_plain(final_low, w_head) * byte_valid
    grad_mid, grad_attn_low, grad_qkv_low, grad_attn_part, grad_norm_mlp = attn_backward(
        after_attn, grad_final, grad_mlp_part, grad_mlp_other, gain_mlp, qkv, w_qkv, w_o
    )
    grad_norm_mlp = grad_norm_mlp.reshape(-1)
    grad_attn_in = tp_sum(grad_attn_part)

    back_attn, grad_norm_attn = rms_back(stream_in, gain_attn, grad_attn_in)
    grad_stream = grad_mid + back_attn
    grad_global = jnp.sum(grad_stream.reshape(patch_total, 8, model_width), axis=1)
    grad_mix_low = (grad_global * valid).astype(jnp.bfloat16)
    grad_normed = dot_plain(grad_mix_low, w_out).reshape(streams, patch_count, inner_width)
    grad_mix_gain = jnp.sum(grad_normed * unit_normed, axis=(0, 1))
    grad_result, grad_gate_in = norm_back(grad_normed * mix_scale)
    grad_z_low = grad_gate_in.reshape(patch_total, inner_width).astype(jnp.bfloat16)
    row_block = model_width // parts
    dealing = after(by_lane(grad_result), bytes_all, group_halves)
    dealt = trade(dealing)
    late_sent = [
        jnp.concatenate([grad_global, part], axis=-1) for part in by_apart(quarters(grad_gate_in))
    ]
    late_got = group_swap(late_sent)
    attn_cut = 1024 if grad_qkv_low.shape[1] > 1024 else 128
    attn_in_late = after(attn_in, dealing)
    attn_cols = grad_qkv_low.shape[1]
    attn_blocks = (
        grad_blocks([(attn_in_late, grad_qkv_low, 0, attn_cut)], 0, True),
        grad_blocks(
            [
                (attn_in_late, grad_qkv_low, attn_cut, attn_cols),
                (grad_attn_low, mixed_low, 0, mixed_low.shape[1]),
                (final_low, grad_logits, 0, head_cols),
            ],
            1,
            True,
        ),
    )
    attn_got = [to_partner(attn_blocks[first][0], first) for first in range(2)]
    dealt = after(dealt, attn_blocks[0][0], attn_blocks[1][0])
    grad_scanned = dealt.reshape(places, width)
    if use_kernel:
        back_sent, conv_grads, head_grads = scan_backward(scan_args, grad_scanned)
        lane_grad = back_sent[:, : scan_width + own_heads]
        scan_params = (
            conv_grads[:4],
            conv_grads[4],
            head_grads[0, :own_heads],
            head_grads[1, :own_heads],
            head_grads[2, :own_heads],
        )
    else:
        scan_grads = scan_back(grad_scanned)
        back_sent = jnp.concatenate(
            [scan_grads[0], jnp.pad(scan_grads[1], ((0, 0), (0, pad_width)))], axis=-1
        )
        lane_grad = jnp.concatenate([scan_grads[0], scan_grads[1]], axis=-1)
        scan_params = scan_grads[2:]
    back_sent = back_sent.reshape(parts, patch_count, -1)
    back_taken = trade(back_sent)
    own_half = after(group_halves, back_sent)
    group_in, group_hidden, group_gate, group_up = group_mlp(
        own_half, swap(own_half, "tp", 1), gain_mlp, group_grad_hidden, w_gate, w_up, place_index
    )
    first_set = grad_blocks(
        [
            (group_final, group_hidden, 0, hidden_part),
            (group_in, group_gate, 0, hidden_part),
        ],
        0,
        True,
    )
    late_got = joined(late_got, first_set[0])
    apart_valid = group_valid.reshape(-1, 1)
    group_mix = (late_got[:, :model_width] * apart_valid).astype(jnp.bfloat16)
    group_z = late_got[:, model_width:]
    late_early = joined(early_got, first_set[0])
    group_u = (late_early[:, :model_width] * gain_global).astype(jnp.bfloat16)
    quarter = inner_width // members
    own_scale = lax.dynamic_slice_in_dim(mix_scale, member * quarter, quarter, 0)
    group_n = (late_early[:, model_width:] * own_scale).astype(jnp.bfloat16)
    attn_far = [
        add_side(after(attn_blocks[first][1], first_set[0]), attn_got[first], 1)
        for first in range(2)
    ]
    attn_crossed = [to_partner(attn_far[first], 1 - first) for first in range(2)]
    mlp_blocks = [
        first_set,
        grad_blocks(
            [
                (group_in, after(group_up, *attn_far), 0, hidden_part),
                (group_mix, group_n, 0, group_n.shape[1]),
                (group_u, group_z, 0, group_z.shape[1]),
            ],
            1,
            True,
        ),
    ]
    mlp_got = [to_partner(mlp_blocks[first][0], first) for first in range(2)]
    back_taken = after(back_taken, mlp_blocks[0][0], mlp_blocks[1][0])
    grad_x = from_lanes(back_taken[..., :width])
    by_stream = back_taken.reshape(streams, lanes, patch_count, -1)
    grad_bc = jnp.sum(by_stream[..., width:scan_width], axis=1)
    grad_dt = from_lanes(back_taken[..., scan_width : scan_width + own_heads])
    grad_dt = jnp.sum(grad_dt.reshape(streams, patch_count, head_total, shared), axis=-1)
    grad_shared = jnp.concatenate([grad_bc, grad_dt], axis=-1).reshape(patch_total, -1)
    grad_proj_low = jnp.concatenate(
        [grad_z_low, grad_x.reshape(patch_total, -1).astype(jnp.bfloat16)]
        + [grad_shared.astype(jnp.bfloat16)],
        axis=-1,
    )
    grad_u_part = dot_trans(grad_proj_low, w_in)
    grad_u = tp_sum(grad_u_part)
    rest = [quarters(columns) for columns in (grad_x, grad_bc, grad_dt)]
    rest_cols = [part.shape[-1] for part in rest]
    rest = after(jnp.concatenate(rest, axis=-1), grad_u_part)
    rest = jnp.pad(rest, ((0, 0), (0, 0), (0, -sum(rest_cols) % 128)))
    rest_blocks = grad_blocks(
        [(group_u, joined(group_swap(by_apart(rest)), grad_u_part), 0, rest.shape[-1])], 0, True
    )
    back_global, grad_norm_global = rms_back(patch_out, gain_global, grad_u)
    grad_patch = grad_global + back_global
    side_count = parts // 2
    my_side = seq_index & 1
    by_block = jnp.moveaxis(grad_patch.reshape(patch_total, parts, row_block), 1, 0)
    by_block = by_block.reshape(side_count, 2, patch_total, row_block)
    same_side = lax.dynamic_index_in_dim(by_block, my_side, 1, keepdims=False)
    other_side = lax.dynamic_index_in_dim(by_block, 1 - my_side, 1, keepdims=False)
    patch_rows = jnp.concatenate([same_side, other_side], axis=-1)
    patch_rows = patch_rows.reshape(side_count, patch_total, 2 * row_block)
    gain_part = grad_norm_global.reshape(-1, 2 * row_block)
    gain_count = gain_part.shape[0]
    patch_sent = jnp.concatenate(
        [patch_rows, jnp.broadcast_to(gain_part, (side_count,) + gain_part.shape)], axis=1
    )
    patch_taken = lax.all_to_all(
        patch_sent, "seq", 0, 0, axis_index_groups=row_side, tiled=True
    )

    mlp_far = [
        add_side(after(mlp_blocks[first][1], patch_sent), mlp_got[first], 1)
        for first in range(2)
    ]
    mlp_crossed = [to_partner(mlp_far[first], 1 - first) for first in range(2)]
    patch_taken = after(patch_taken, rest_blocks[0], *mlp_far)
    gain_side = jnp.sum(patch_taken[:, patch_total:], axis=0)
    patch_cols = patch_taken[:, :patch_total].reshape(-1, 2 * row_block)
    patch_far = patch_far_grad(patch_cols, gain_side, bytes_all)
    small = (
        scan_params[0][:, :width],
        scan_params[1][:width],
        scan_params[0][:, width:],
        scan_params[1][width:],
        scan_params[2],
        scan_params[3],
        scan_params[4],
        grad_mix_gain,
        grad_norm_attn,
        grad_norm_mlp,
    )
    small_count = sum(part.size for part in small)
    flat = after(jnp.concatenate([part.reshape(-1) for part in small]), patch_far)
    flat = jnp.pad(flat, (0, -small_count % 1024)).reshape(1, -1, 128)
    pieces = trade(jnp.broadcast_to(flat, (parts,) + flat.shape[1:])).reshape(parts, -1)
    by_small, at = [], 0
    for part in small:
        got = pieces[:, at : at + part.size].reshape((parts,) + part.shape)
        by_small.append(got)
        at += part.size

    def lane_cols(got):
        joined = jnp.sum(got.reshape((streams, lanes) + got.shape[1:]), axis=0)
        return jnp.moveaxis(joined, 0, -2).reshape(joined.shape[1:-1] + (-1,))

    def lane_heads(got):
        joined = jnp.sum(got.reshape(streams, lanes, -1), axis=0)
        return jnp.sum(joined.reshape(head_total, shared), axis=-1)

    small_sums = [
        jnp.concatenate([lane_cols(by_small[0]), jnp.sum(by_small[2], axis=0)], axis=-1),
        jnp.concatenate([lane_cols(by_small[1]), jnp.sum(by_small[3], axis=0)], axis=-1),
        lane_heads(by_small[4]),
        lane_heads(by_small[5]),
        lane_heads(by_small[6]),
    ] + [jnp.sum(got, axis=0) for got in by_small[7:]]

    patch_got = to_partner(patch_far, 0)

    high = (seq_index // QUAD).astype(jnp.int32).reshape(1)
    attn_near = near_sums(
        [
            (after(attn_blocks[first][1], patch_far), attn_got[first], attn_crossed[first])
            for first in range(2)
        ],
        high,
    )
    attn_high = [
        swap(attn_near[apart], "seq", QUAD * apart) for apart in range(1, parts // QUAD)
    ]
    rest_got = to_partner(after(rest_blocks[0], patch_far), 0)
    start = jnp.zeros((1,), jnp.int32)
    mlp_near = [
        near_sums(
            [(after(mlp_blocks[first][1], attn_near, patch_got), mlp_got[first], mlp_crossed[first])],
            start,
        )
        for first in range(2)
    ]
    final_attn = attn_near[0]
    for got in attn_high:
        final_attn = final_attn + after(got, *mlp_near)
    rest_far = add_side(after(rest_blocks[1], *mlp_near), rest_got, 1)
    rest_crossed = to_partner(rest_far, 1)
    rest_near = near_sums(
        [(after(rest_blocks[1], final_attn), rest_got, rest_crossed)], start
    )
    mlp_finals = [
        jnp.moveaxis(group_trade(part), 0, 1) for part in mlp_near + [rest_near]
    ]
    def final_cols(final, low, count):
        return final[..., low : low + count].reshape(row_block, -1)

    final_down = final_cols(mlp_finals[0], 0, hidden_part)
    final_gate = final_cols(mlp_finals[0], hidden_part, hidden_part)
    final_up = final_cols(mlp_finals[1], 0, hidden_part)
    final_out = final_cols(mlp_finals[1], hidden_part, quarter)
    final_z = final_cols(mlp_finals[1], hidden_part + quarter, quarter)
    final_x = final_cols(mlp_finals[2], 0, rest_cols[0])
    final_bc = final_cols(mlp_finals[2], rest_cols[0], rest_cols[1])
    final_dt = final_cols(mlp_finals[2], rest_cols[0] + rest_cols[1], rest_cols[2])
    final_patch = patch_grad(patch_cols, patch_got, bytes_all)
    norm_global_sum = (gain_side + patch_got[row_block:, : 2 * row_block]).reshape(-1)
    grad_bytes = bytes_grad(after(grad_patch, patch_far), w_patch, grad_stream)
    grad_bytes = grad_bytes.reshape(streams, local_rows, feature)

    qkv_cols, o_cols = w_qkv.shape[1], w_o.shape[1]
    return (
        logits.reshape(streams, local_rows, head_cols),
        grad_bytes,
        final_patch,
        norm_global_sum,
        jnp.concatenate([final_z, final_x, final_bc, final_dt], axis=1),
        small_sums[0],
        small_sums[1],
        small_sums[2],
        small_sums[3],
        small_sums[4],
        small_sums[5],
        final_out,
        small_sums[6],
        final_attn[:, :qkv_cols],
        final_attn[:, qkv_cols : qkv_cols + o_cols],
        small_sums[7],
        final_gate,
        final_up,
        final_down,
        final_attn[:, qkv_cols + o_cols :],
    )


def solution(mesh):
    in_specs = (
        P(None, "seq", None),
        P(),
        P(None, "tp"),
        P(),
        P(None, "tp"),
        P(None, "tp"),
        P("tp"),
        P("tp"),
        P("tp"),
        P("tp"),
        P("tp"),
        P(None, "tp"),
        P(),
        P(None, "tp"),
        P(None, "tp"),
        P(),
        P(None, "tp"),
        P(None, "tp"),
        P(None, "tp"),
        P(None, "tp"),
        P(None, "seq", "tp"),
    )
    out_specs = (
        P(None, "seq", "tp"),
        P(None, "seq", "tp"),
        P("seq", "tp"),
        P(),
        P("seq", "tp"),
        P(None, "tp"),
        P("tp"),
        P("tp"),
        P("tp"),
        P("tp"),
        P("tp"),
        P("seq", "tp"),
        P(),
        P("seq", "tp"),
        P("seq", "tp"),
        P(),
        P("seq", "tp"),
        P("seq", "tp"),
        P("seq", "tp"),
        P("seq", "tp"),
    )
    return jax.shard_map(body, mesh=mesh, in_specs=in_specs, out_specs=out_specs, check_vma=False)
```

profile of v0, /device:TPU:0, one launch (start us, length us, event | category | flops | bytes accessed | tf_op | source)
XLA Modules:
  0.0 661.2 jit_solution(15931748664554668156)
XLA Ops:
  7.3 9.2 %shard_map.356 = (f32[64,4096]{1,0:T(8,128)}, f32[64,1024]{1,0:T(8,128)}) custom-call(s32[1]{0:T(128)} %bitcast.core_ref, bf16[512,1024]{1,0:T(8,128)(2,1)} %bitcast.251, bf16[1024,4096]{1,0:T(8,128)(2,1)} %weight_ref.5), custom_call_target="tpu_custom_call" | custom-call | flops 1024 | bytes 1024 | tf_op jit(solution)/shard_map/pallas_call | solution.py:910
  25.8 8.2 %all-to-all-start = ((f32[16,32,512]{2,1,0:T(8,128)}), f32[16,32,512]{2,1,0:T(8,128)S(1)}, u32[]{:S(2)}, u32[]{:S(2)}) async-start(f32[16,32,512]{2,1,0:T(8,128)} %select_maximum_fusion), calls=%async_computation | async-start | bytes 2097152 | tf_op jit(solution)/shard_map/all_to_all | solution.py:362
  47.9 26.2 %all-to-all-done = f32[16,32,512]{2,1,0:T(8,128)S(1)} async-done(((f32[16,32,512]{2,1,0:T(8,128)}), f32[16,32,512]{2,1,0:T(8,128)S(1)}, u32[]{:S(2)}, u32[]{:S(2)}) %all-to-all-start) | async-done | bytes 1048608 | tf_op jit(solution)/shard_map/all_to_all | solution.py:362
  84.5 30.8 %collective-permute-done.2 = f32[512,128]{1,0:T(8,128)} collective-permute-done((f32[512,128]{1,0:T(8,128)}, f32[512,128]{1,0:T(8,128)}, u32[]{:S(2)}, u32[]{:S(2)}) %collective-permute-start.2) | collective-permute-done | bytes 262176 | tf_op jit(solution)/shard_map/ppermute | solution.py:65
  124.6 10.5 %shard_map.358 = (bf16[2048,1024]{1,0:T(8,128)(2,1)}, f32[2048,512]{1,0:T(8,128)}, f32[512,1024]{1,0:T(8,128)}, bf16[512,1024]{1,0:T(8,128)(2,1)}) custom-call(s32[1]{0:T(128)} %bitcast.22.member_ref.index_ref, f32[2048,128]{1,0:T(8,128)} %copy-done.13, f32[2048,128]{1,0:T(8,128)} %collective-permute-done.4.other_ref, f32[2048,1]{1,0:T(8,128)} %broadcast_in_dim.74.mask_ref, ...), custom_call_target="tpu_custom_call" | custom-call | flops 1024 | bytes 1024 | tf_op jit(solution)/shard_map/pallas_call | solution.py:976
  148.1 7.8 %shard_map.359 = (f32[512,1024]{1,0:T(8,128)}, bf16[512,1024]{1,0:T(8,128)(2,1)}, bf16[512,1536]{1,0:T(8,128)(2,1)}, bf16[512,512]{1,0:T(8,128)(2,1)}, f32[512,1024]{1,0:T(8,128)}) custom-call(bf16[512,1024]{1,0:T(8,128)(2,1)} %bitcast.252, f32[64,1024]{1,0:T(8,128)} %multiply_add_fusion.patch_ref, f32[1,1024]{1,0:T(1,128)} %bitcast.319, ...), custom_call_target="tpu_custom_call" | custom-call | flops 1024 | bytes 1024 | tf_op jit(solution)/shard_map/pallas_call | solution.py:645
  167.0 15.2 %shard_map.361 = (bf16[512,2048]{1,0:T(8,128)(2,1)}, bf16[512,2048]{1,0:T(8,128)(2,1)}, bf16[512,2048]{1,0:T(8,128)(2,1)}, f32[512,1024]{1,0:T(8,128)}) custom-call(bf16[512,1024]{1,0:T(8,128)(2,1)} %get-tuple-element.115.in_ref, f32[512,2048]{1,0:T(8,128)} %fusion.45.grad_ref, bf16[1024,2048]{1,0:T(8,128)(2,1)} %gate_w_ref.3, bf16[1024,2048]{1,0:T(8,128)(2,1)} %up_w_ref.3), custom_call_target="tpu_custom_call" | custom-call | flops 1024 | bytes 1024 | tf_op jit(solution)/shard_map/pallas_call | solution.py:853
  190.4 11.5 %shard_map.362 = (f32[512,1024]{1,0:T(8,128)}, bf16[512,1024]{1,0:T(8,128)(2,1)}, bf16[512,1536]{1,0:T(8,128)(2,1)}, f32[512,1024]{1,0:T(8,128)}, f32[1,1024]{1,0:T(1,128)}) custom-call(f32[512,1024]{1,0:T(8,128)} %get-tuple-element.112.x_ref, f32[512,1024]{1,0:T(8,128)} %get-tuple-element.119.final_ref, f32[512,1024]{1,0:T(8,128)} %get-tuple-element.117.own_ref, ...), custom_call_target="tpu_custom_call" | custom-call | flops 1024 | bytes 1024 | tf_op jit(solution)/shard_map/pallas_call | solution.py:749
  220.8 63.6 %all-to-all-done.2.own_ref = f32[4,512,512]{2,1,0:T(8,128)} async-done(((f32[4,512,512]{2,1,0:T(8,128)}), f32[4,512,512]{2,1,0:T(8,128)}, u32[]{:S(2)}, u32[]{:S(2)}) %all-to-all-start.2) | async-done | bytes 4194336 | tf_op jit(solution)/shard_map/all_to_all | solution.py:90
  300.5 8.0 %shard_map.364 = (f32[2,4,64,1152]{3,2,1,0:T(8,128)}, f32[2,4,64,1152]{3,2,1,0:T(8,128)}) custom-call(s32[1]{0:T(128)} %bitcast.39.member_ref, bf16[512,1024]{1,0:T(8,128)(2,1)} %get-tuple-element.125.refs_0_, bf16[512,1024]{1,0:T(8,128)(2,1)} %get-tuple-element.128.refs_1_, bf16[512,1024]{1,0:T(8,128)(2,1)} %add_convert_fusion.refs_2_, ...), custom_call_target="tpu_custom_call" | custom-call | flops 1024 | bytes 1024 | tf_op jit(solution)/shard_map/pallas_call | solution.py:201
  309.2 10.2 %shard_map.365 = (f32[512,512]{1,0:T(8,128)}, f32[8,384]{1,0:T(8,128)}, f32[8,128]{1,0:T(8,128)}) custom-call(f32[512,512]{1,0:T(8,128)} %bitcast.249, f32[512,8]{1,0:T(8,128)} %copy.143.same_ref, f32[8,384]{1,0:T(8,128)} %maximum_maximum_fusion.conv_ref, f32[8,128]{1,0:T(8,128)} %stack.87.head_ref, s32[512,1]{1,0:T(8,128)} %copy.144.seg_col, ...), custom_call_target="tpu_custom_call" | custom-call | flops 1024 | bytes 1024 | tf_op jit(solution)/shard_map/pallas_call | solution.py:548
  339.2 12.3 %shard_map.366 = (bf16[2048,1024]{1,0:T(8,128)(2,1)}, bf16[2048,512]{1,0:T(8,128)(2,1)}, bf16[2048,512]{1,0:T(8,128)(2,1)}, bf16[2048,512]{1,0:T(8,128)(2,1)}) custom-call(s32[2]{0:T(128)} %pad_add_fusion.place_ref, f32[4,512,512]{2,1,0:T(8,128)} %all-to-all-done.2.own_ref, f32[4,512,512]{2,1,0:T(8,128)} %collective-permute-done.11.other_ref, ...), custom_call_target="tpu_custom_call" | custom-call | flops 1024 | bytes 1024 | tf_op jit(solution)/shard_map/pallas_call | solution.py:1029
  351.6 10.9 %shard_map.367 = (f32[2,4,64,1024]{3,2,1,0:T(8,128)}, f32[2,4,64,1024]{3,2,1,0:T(8,128)}) custom-call(s32[1]{0:T(128)} %bitcast.39.member_ref, bf16[2048,1024]{1,0:T(8,128)(2,1)} %get-tuple-element.133.refs_0_, bf16[2048,1024]{1,0:T(8,128)(2,1)} %get-tuple-element.135.refs_1_.refs_0_, bf16[2048,512]{1,0:T(8,128)(2,1)} %get-tuple-element.136.refs_2_, ...), custom_call_target="tpu_custom_call" | custom-call | flops 1024 | bytes 1024 | tf_op jit(solution)/shard_map/pallas_call | solution.py:201
  365.1 11.4 %collective-permute-done.18.refs_1_ = f32[2,4,64,1024]{3,2,1,0:T(8,128)S(1)} collective-permute-done((f32[2,4,64,1024]{3,2,1,0:T(8,128)}, f32[2,4,64,1024]{3,2,1,0:T(8,128)S(1)}, u32[]{:S(2)}, u32[]{:S(2)}) %collective-permute-start.18) | collective-permute-done | bytes 2097184 | tf_op jit(solution)/shard_map/ppermute | solution.py:65
  391.7 7.2 %collective-permute-done.16 = f32[64,1280]{1,0:T(8,128)S(1)} collective-permute-done((f32[64,1280]{1,0:T(8,128)S(1)}, f32[64,1280]{1,0:T(8,128)S(1)}, u32[]{:S(2)}, u32[]{:S(2)}) %collective-permute-start.16) | collective-permute-done | bytes 327712 | tf_op jit(solution)/shard_map/ppermute | solution.py:65
  402.3 9.0 %shard_map.370 = (f32[2,4,64,1024]{3,2,1,0:T(8,128)}, f32[2,4,64,1024]{3,2,1,0:T(8,128)}) custom-call(s32[1]{0:T(128)} %bitcast.39.member_ref, bf16[2048,1024]{1,0:T(8,128)(2,1)} %get-tuple-element.135.refs_1_.refs_0_, bf16[256,1024]{1,0:T(8,128)(2,1)} %fusion.1.refs_1_, bf16[256,1024]{1,0:T(8,128)(2,1)} %fusion.refs_2_.refs_0_, ...), custom_call_target="tpu_custom_call" | custom-call | flops 1024 | bytes 1024 | tf_op jit(solution)/shard_map/pallas_call | solution.py:201
  431.7 15.8 %all-to-all-start.5 = ((f32[8,72,128]{2,1,0:T(8,128)}), f32[8,72,128]{2,1,0:T(8,128)S(1)}, u32[]{:S(2)}, u32[]{:S(2)}) async-start(f32[8,72,128]{2,1,0:T(8,128)} %pad_maximum_fusion.12), calls=%async_computation.5 | async-start | bytes 589824 | tf_op jit(solution)/shard_map/all_to_all | solution.py:1440
  451.9 6.8 %collective-permute-done.23 = f32[64,384]{1,0:T(8,128)S(1)} collective-permute-done((f32[64,384]{1,0:T(8,128)S(1)}, f32[64,384]{1,0:T(8,128)S(1)}, u32[]{:S(2)}, u32[]{:S(2)}) %collective-permute-start.23) | collective-permute-done | bytes 98336 | tf_op jit(solution)/shard_map/ppermute | solution.py:65
  509.2 13.2 %collective-permute-start.32 = (f32[64,2176]{1,0:T(8,128)}, f32[64,2176]{1,0:T(8,128)}, u32[]{:S(2)}, u32[]{:S(2)}) collective-permute-start(f32[64,2176]{1,0:T(8,128)} %get-tuple-element.205), channel_id=1, source_target_pairs={{0,16},{2,18},{4,20},{6,22},{8,24},{10,26},{12,28},{14,30},{16,0},... | collective-permute-start | bytes 1671176 | tf_op jit(solution)/shard_map/ppermute | solution.py:65
  523.5 14.1 %collective-permute-start.30 = (f32[64,2176]{1,0:T(8,128)}, f32[64,2176]{1,0:T(8,128)}, u32[]{:S(2)}, u32[]{:S(2)}) collective-permute-start(f32[64,2176]{1,0:T(8,128)} %get-tuple-element.203), channel_id=1, source_target_pairs={{0,8},{2,10},{4,12},{6,14},{8,0},{10,2},{12,4},{14,6},{16,24},{18,... | collective-permute-start | bytes 1671176 | tf_op jit(solution)/shard_map/ppermute | solution.py:65
  550.8 8.5 %collective-permute-done.32 = f32[64,2176]{1,0:T(8,128)} collective-permute-done((f32[64,2176]{1,0:T(8,128)}, f32[64,2176]{1,0:T(8,128)}, u32[]{:S(2)}, u32[]{:S(2)}) %collective-permute-start.32) | collective-permute-done | bytes 557088 | tf_op jit(solution)/shard_map/ppermute | solution.py:65
  575.9 26.2 %all_to_all.50 = f32[4,64,384]{2,1,0:T(8,128)S(1)} all-to-all(f32[4,64,384]{2,1,0:T(8,128)} %shard_map.381), channel_id=1, replica_groups={{0,8,16,24},{2,10,18,26},{4,12,20,28},{6,14,22,30},{1,9,17,25},{3,11,19..., dimensions={0} | all-to-all | bytes 786432 | tf_op jit(solution)/shard_map/all_to_all | solution.py:90
  607.0 12.4 %shard_map.375 = f32[512,512]{1,0:T(8,128)} custom-call(s32[1]{0:T(128)} %bitcast.core_ref, f32[64,1024]{1,0:T(8,128)} %copy-done.21, bf16[1024,4096]{1,0:T(8,128)(2,1)} %weight_ref.5, f32[512,1024]{1,0:T(8,128)} %get-tuple-element.196.stream_ref), custom_call_target="tpu_custom_call" | custom-call | flops 1024 | bytes 1024 | tf_op jit(solution)/shard_map/pallas_call | solution.py:1076
  633.7 9.1 %shard_map.376 = f32[64,4096]{1,0:T(8,128)} custom-call(f32[512,128]{1,0:T(8,128)} %bitcast.262, f32[512,4096]{1,0:T(8,128)} %all-gather.2.cloned.1.call-done.bytes_ref.refs_0_.refs_1_.refs_2_.refs_3_.refs_4_.refs_5_.refs_6_.refs_7_, f32[512,4096]{1,0:T(8,128)} %all-gather.2.cloned.1.call-done.bytes_ref.refs_0_.refs_1_.refs_2_.refs_3_.refs_4_.refs_5_.refs_6_.refs_7_, ...), custom_call_target="tpu_custom_call" | custom-call | flops 1024 | bytes 1024 | tf_op jit(solution)/shard_map/pallas_call | solution.py:347
  (408 shorter events, 287.6 us)
Async XLA Ops:
  7.2 277.2 %all-gather.2.cloned.1.call-start = ((), (), s32[]{:S(2)}) async-start(), calls=%async_computation.10 | async-start | bytes 9437184 | tf_op jit(solution)/shard_map/all_gather | solution.py:1201
  25.8 48.3 %all-to-all-start = ((f32[16,32,512]{2,1,0:T(8,128)}), f32[16,32,512]{2,1,0:T(8,128)S(1)}, u32[]{:S(2)}, u32[]{:S(2)}) async-start(f32[16,32,512]{2,1,0:T(8,128)} %select_maximum_fusion), calls=%async_computation | async-start | bytes 2097152 | tf_op jit(solution)/shard_map/all_to_all | solution.py:362
  34.8 49.7 %collective-permute-start.3 = (f32[512,128]{1,0:T(8,128)}, f32[512,128]{1,0:T(8,128)}, u32[]{:S(2)}, u32[]{:S(2)}) collective-permute-start(f32[512,128]{1,0:T(8,128)} %bitcast_convert_fusion), channel_id=1, source_target_pairs={{0,24},{2,26},{4,28},{6,30},{8,16},{10,18},{12,20},{14,22},{16,8},... | collective-permute-start | bytes 786440 | tf_op jit(solution)/shard_map/ppermute | solution.py:65
  38.5 76.8 %collective-permute-start.2 = (f32[512,128]{1,0:T(8,128)}, f32[512,128]{1,0:T(8,128)}, u32[]{:S(2)}, u32[]{:S(2)}) collective-permute-start(f32[512,128]{1,0:T(8,128)} %bitcast_convert_fusion), channel_id=1, source_target_pairs={{0,16},{2,18},{4,20},{6,22},{8,24},{10,26},{12,28},{14,30},{16,0},... | collective-permute-start | bytes 786440 | tf_op jit(solution)/shard_map/ppermute | solution.py:65
  38.5 76.8 %collective-permute-start.1 = (f32[512,128]{1,0:T(8,128)}, f32[512,128]{1,0:T(8,128)}, u32[]{:S(2)}, u32[]{:S(2)}) collective-permute-start(f32[512,128]{1,0:T(8,128)} %bitcast_convert_fusion), channel_id=1, source_target_pairs={{0,8},{2,10},{4,12},{6,14},{8,0},{10,2},{12,4},{14,6},{16,24},{18,... | collective-permute-start | bytes 786440 | tf_op jit(solution)/shard_map/ppermute | solution.py:65
  185.0 99.4 %all-to-all-start.2 = ((f32[4,512,512]{2,1,0:T(8,128)}), f32[4,512,512]{2,1,0:T(8,128)}, u32[]{:S(2)}, u32[]{:S(2)}) async-start(f32[4,512,512]{2,1,0:T(8,128)} %broadcast_in_dim.70), calls=%async_computation.2 | async-start | bytes 8388608 | tf_op jit(solution)/shard_map/all_to_all | solution.py:90
  210.8 80.4 %collective-permute-start.8 = (f32[512,1024]{1,0:T(8,128)}, f32[512,1024]{1,0:T(8,128)}, u32[]{:S(2)}, u32[]{:S(2)}) collective-permute-start(f32[512,1024]{1,0:T(8,128)} %fusion.47), channel_id=1, source_target_pairs={{0,1},{1,0},{2,3},{3,2},{4,5},{5,4},{6,7},{7,6},{8,9},{9,8},{10,11... | collective-permute-start | bytes 6291464 | tf_op jit(solution)/shard_map/ppermute | solution.py:65
  319.4 57.1 %collective-permute-start.18 = (f32[2,4,64,1024]{3,2,1,0:T(8,128)}, f32[2,4,64,1024]{3,2,1,0:T(8,128)S(1)}, u32[]{:S(2)}, u32[]{:S(2)}) collective-permute-start(f32[2,4,64,1024]{3,2,1,0:T(8,128)} %get-tuple-element.127), channel_id=1, source_target_pairs={{0,2},{2,0},{4,6},{6,4},{8,10},{10,8},{12,14},{14,12},{16,18},{18,... | collective-permute-start | bytes 6291464 | tf_op jit(solution)/shard_map/ppermute | solution.py:65
  321.4 64.2 %collective-permute-start.19 = (f32[2,4,64,1152]{3,2,1,0:T(8,128)}, f32[2,4,64,1152]{3,2,1,0:T(8,128)}, u32[]{:S(2)}, u32[]{:S(2)}) collective-permute-start(f32[2,4,64,1152]{3,2,1,0:T(8,128)} %get-tuple-element.130), channel_id=1, source_target_pairs={{0,4},{2,6},{4,0},{6,2},{8,12},{10,14},{12,8},{14,10},{16,20},{18,... | collective-permute-start | bytes 7077896 | tf_op jit(solution)/shard_map/ppermute | solution.py:65
  329.8 35.2 %collective-permute-start.13 = (f32[64,1280]{1,0:T(8,128)}, f32[64,1280]{1,0:T(8,128)}, u32[]{:S(2)}, u32[]{:S(2)}) collective-permute-start(f32[64,1280]{1,0:T(8,128)} %get-tuple-element.228), channel_id=1, source_target_pairs={{0,16},{2,18},{4,20},{6,22},{8,24},{10,26},{12,28},{14,30},{16,0},... | collective-permute-start | bytes 983048 | tf_op jit(solution)/shard_map/ppermute | solution.py:65
  333.4 77.9 %all-to-all-start.4 = ((f32[16,32,512]{2,1,0:T(8,128)}), f32[16,32,512]{2,1,0:T(8,128)S(1)}, u32[]{:S(2)}, u32[]{:S(2)}) async-start(f32[16,32,512]{2,1,0:T(8,128)} %bitcast.282), calls=%async_computation.4 | async-start | bytes 2097152 | tf_op jit(solution)/shard_map/all_to_all | solution.py:362
  337.3 54.5 %collective-permute-start.15 = (f32[64,1280]{1,0:T(8,128)}, f32[64,1280]{1,0:T(8,128)S(1)}, u32[]{:S(2)}, u32[]{:S(2)}) collective-permute-start(f32[64,1280]{1,0:T(8,128)} %get-tuple-element.219), channel_id=1, source_target_pairs={{0,8},{2,10},{4,12},{6,14},{8,0},{10,2},{12,4},{14,6},{16,24},{18,... | collective-permute-start | bytes 983048 | tf_op jit(solution)/shard_map/ppermute | solution.py:65
  362.5 36.5 %collective-permute-start.16 = (f32[64,1280]{1,0:T(8,128)S(1)}, f32[64,1280]{1,0:T(8,128)S(1)}, u32[]{:S(2)}, u32[]{:S(2)}) collective-permute-start(f32[64,1280]{1,0:T(8,128)S(1)} %copy-done.41), channel_id=1, source_target_pairs={{0,16},{2,18},{4,20},{6,22},{8,24},{10,26},{12,28},{14,30},{16,0},... | collective-permute-start | bytes 983048 | tf_op jit(solution)/shard_map/ppermute | solution.py:65
  412.8 62.2 %collective-permute-start.24 = (f32[2,4,64,1024]{3,2,1,0:T(8,128)}, f32[2,4,64,1024]{3,2,1,0:T(8,128)}, u32[]{:S(2)}, u32[]{:S(2)}) collective-permute-start(f32[2,4,64,1024]{3,2,1,0:T(8,128)} %get-tuple-element.138), channel_id=1, source_target_pairs={{0,2},{2,0},{4,6},{6,4},{8,10},{10,8},{12,14},{14,12},{16,18},{18,... | collective-permute-start | bytes 6291464 | tf_op jit(solution)/shard_map/ppermute | solution.py:65
  413.0 67.3 %collective-permute-start.25 = (f32[2,4,64,1024]{3,2,1,0:T(8,128)}, f32[2,4,64,1024]{3,2,1,0:T(8,128)S(1)}, u32[]{:S(2)}, u32[]{:S(2)}) collective-permute-start(f32[2,4,64,1024]{3,2,1,0:T(8,128)} %get-tuple-element.153), channel_id=1, source_target_pairs={{0,4},{2,6},{4,0},{6,2},{8,12},{10,14},{12,8},{14,10},{16,20},{18,... | collective-permute-start | bytes 6291464 | tf_op jit(solution)/shard_map/ppermute | solution.py:65
  421.2 76.0 %collective-permute-start.27 = (f32[4,64,1024]{2,1,0:T(8,128)}, f32[4,64,1024]{2,1,0:T(8,128)}, u32[]{:S(2)}, u32[]{:S(2)}) collective-permute-start(f32[4,64,1024]{2,1,0:T(8,128)} %shard_map.368), channel_id=1, source_target_pairs={{0,4},{2,6},{4,0},{6,2},{8,12},{10,14},{12,8},{14,10},{16,20},{18,... | collective-permute-start | bytes 3145736 | tf_op jit(solution)/shard_map/ppermute | solution.py:65
  422.7 76.4 %collective-permute-start.28 = (f32[4,64,1152]{2,1,0:T(8,128)}, f32[4,64,1152]{2,1,0:T(8,128)}, u32[]{:S(2)}, u32[]{:S(2)}) collective-permute-start(f32[4,64,1152]{2,1,0:T(8,128)} %shard_map.369), channel_id=1, source_target_pairs={{0,2},{2,0},{4,6},{6,4},{8,10},{10,8},{12,14},{14,12},{16,18},{18,... | collective-permute-start | bytes 3538952 | tf_op jit(solution)/shard_map/ppermute | solution.py:65
  431.7 55.7 %all-to-all-start.5 = ((f32[8,72,128]{2,1,0:T(8,128)}), f32[8,72,128]{2,1,0:T(8,128)S(1)}, u32[]{:S(2)}, u32[]{:S(2)}) async-start(f32[8,72,128]{2,1,0:T(8,128)} %pad_maximum_fusion.12), calls=%async_computation.5 | async-start | bytes 589824 | tf_op jit(solution)/shard_map/all_to_all | solution.py:1440
  497.1 49.9 %collective-permute-start.29 = (f32[4,64,1024]{2,1,0:T(8,128)}, f32[4,64,1024]{2,1,0:T(8,128)}, u32[]{:S(2)}, u32[]{:S(2)}) collective-permute-start(f32[4,64,1024]{2,1,0:T(8,128)} %shard_map.373), channel_id=1, source_target_pairs={{0,2},{2,0},{4,6},{6,4},{8,10},{10,8},{12,14},{14,12},{16,18},{18,... | collective-permute-start | bytes 3145736 | tf_op jit(solution)/shard_map/ppermute | solution.py:65
  497.3 62.5 %collective-permute-start.34 = (f32[2,4,64,384]{3,2,1,0:T(8,128)}, f32[2,4,64,384]{3,2,1,0:T(8,128)S(1)}, u32[]{:S(2)}, u32[]{:S(2)}) collective-permute-start(f32[2,4,64,384]{3,2,1,0:T(8,128)} %get-tuple-element.176), channel_id=1, source_target_pairs={{0,2},{2,0},{4,6},{6,4},{8,10},{10,8},{12,14},{14,12},{16,18},{18,... | collective-permute-start | bytes 2359304 | tf_op jit(solution)/shard_map/ppermute | solution.py:65
  506.5 44.3 %collective-permute-start.33 = (f32[64,2176]{1,0:T(8,128)}, f32[64,2176]{1,0:T(8,128)}, u32[]{:S(2)}, u32[]{:S(2)}) collective-permute-start(f32[64,2176]{1,0:T(8,128)} %get-tuple-element.204), channel_id=1, source_target_pairs={{0,24},{2,26},{4,28},{6,30},{8,16},{10,18},{12,20},{14,22},{16,8},... | collective-permute-start | bytes 1671176 | tf_op jit(solution)/shard_map/ppermute | solution.py:65
  509.2 50.0 %collective-permute-start.32 = (f32[64,2176]{1,0:T(8,128)}, f32[64,2176]{1,0:T(8,128)}, u32[]{:S(2)}, u32[]{:S(2)}) collective-permute-start(f32[64,2176]{1,0:T(8,128)} %get-tuple-element.205), channel_id=1, source_target_pairs={{0,16},{2,18},{4,20},{6,22},{8,24},{10,26},{12,28},{14,30},{16,0},... | collective-permute-start | bytes 1671176 | tf_op jit(solution)/shard_map/ppermute | solution.py:65
  523.5 35.7 %collective-permute-start.30 = (f32[64,2176]{1,0:T(8,128)}, f32[64,2176]{1,0:T(8,128)}, u32[]{:S(2)}, u32[]{:S(2)}) collective-permute-start(f32[64,2176]{1,0:T(8,128)} %get-tuple-element.203), channel_id=1, source_target_pairs={{0,8},{2,10},{4,12},{6,14},{8,0},{10,2},{12,4},{14,6},{16,24},{18,... | collective-permute-start | bytes 1671176 | tf_op jit(solution)/shard_map/ppermute | solution.py:65
  538.5 37.4 %all-to-all-start.8 = ((f32[16,40,128]{2,1,0:T(8,128)}), f32[16,40,128]{2,1,0:T(8,128)}, u32[]{:S(2)}, u32[]{:S(2)}) async-start(f32[16,40,128]{2,1,0:T(8,128)} %broadcast_in_dim.73), calls=%async_computation.8 | async-start | bytes 655360 | tf_op jit(solution)/shard_map/all_to_all | solution.py:362
  (81 other events, 1405.5 us)
Sparse Core Ops, SparseCore 0:
  17.1 167.9 all-gather.1
where the time goes:
time: 672 us; the launch traced here: 661 us
  waiting for transfers between devices  189 us (28%)
  Pallas kernels  187 us (28%)
  starting transfers between devices  125 us (19%)
  local copies, waits for them, and re-layouts  49.1 us (7%)
  other arithmetic  47.5 us (7%)
  blocking collectives  26.2 us (4%)
  matrix products  22.2 us (3%)
  between operations  15.7 us (2%)
    ppermute x36, waiting for transfers between devices, swap(): lax.ppermute(block, axis, [(i, i ^ mask) for i in range(lax.axis_size(axi...  90.1 us
    ppermute x36, starting transfers between devices, swap(): lax.ppermute(block, axis, [(i, i ^ mask) for i in range(lax.axis_size(axi...  70.5 us
    all_to_all x3, waiting for transfers between devices, group_trade(): lax.all_to_all(blocks, 'seq', 0, 0, axis_index_groups=members, tiled=True)  70.1 us
    pallas_call x5, Pallas kernels, grad_blocks(): pl.pallas_call(partial(grad_blocks_kernel, pairs, first, relative, rows),...  37.6 us
    all_to_all x5, waiting for transfers between devices, trade(): return lax.all_to_all(blocks, 'seq', 0, 0, tiled=True)  26.2 us
    all_to_all x1, blocking collectives, group_trade(): lax.all_to_all(blocks, 'seq', 0, 0, axis_index_groups=members, tiled=True)  26.2 us
    all_to_all x5, starting transfers between devices, trade(): return lax.all_to_all(blocks, 'seq', 0, 0, tiled=True)  26.1 us
    pallas_call x5, Pallas kernels, add_side(): pl.pallas_call(add_kernel, grid_spec=pltpu.PrefetchScalarGridSpec(num_sca...  17.5 us
  transfers between devices with their start and end apart: 46, of which 22 were waited for; matrix products, arithmetic and copies ran while one was open for 16% of the time, Pallas kernels for 25%

commit v1 on v0

--- a/solution.py
+++ b/solution.py
@@ -961,10 +961,10 @@
         mine_low_ref[...] = low
 
 
-def final_grads(own, other, mask, own_head, other_head, w_down, member):
+def final_grads(own, other, mask, own_head, other_head, w_down, member, count):
     rows, cols = own.shape
     width = own_head.shape[0]
-    block = rows // group_size()
+    block = rows // count
     units = w_down.shape[1] // group_size()
     f32, bf16 = jnp.float32, jnp.bfloat16
 
@@ -977,7 +977,7 @@
         final_kernel,
         grid_spec=pltpu.PrefetchScalarGridSpec(
             num_scalar_prefetch=1,
-            grid=(group_size(),),
+            grid=(count,),
             in_specs=[by_rows(cols), by_rows(cols), by_rows(1), head, head]
             + [pl.BlockSpec((width, units), lambda i, ref: (0, ref[0]))],
             out_specs=[by_rows(width), by_rows(units), mine, mine],
@@ -1195,13 +1195,27 @@
         axis=-1,
     )
     taken = trade(sent)
+    grad_logits = raw_logits * byte_valid.astype(jnp.bfloat16)
+    unused, unused_part, grad_final, grad_mlp_low = final_grads(
+        after(raw_wide, sent),
+        swap(raw_wide, "tp", 1),
+        byte_valid,
+        w_head,
+        other_head,
+        w_down,
+        place_index,
+        1,
+    )
+    grad_hidden = dot_plain(grad_mlp_low, w_down)
+    hidden_part = w_gate.shape[1] // members
+
     row_side = [
         [device for device in range(parts) if (device & 1) == side] for side in range(2)
     ]
     bytes_all = lax.all_gather(
         bytes_wide, "seq", axis=0, axis_index_groups=row_side, tiled=True
     )
-    taken = after(taken, bytes_wide).reshape(places, -1)
+    taken = after(taken, bytes_wide, grad_hidden).reshape(places, -1)
     scan_width = width + channels - inner_width
 
     def own_cols(param):
@@ -1242,24 +1256,7 @@
         )
         scanned, scan_back = jax.vjp(partial(scan_heads, seg_stream, head_size), *scan_args)
     result = trade(scanned.reshape(parts, patch_count, width))
-    group_raw = jnp.concatenate(
-        [raw_wide] + [after(raw, scanned) for raw in apart_raw], axis=0
-    )
-    other_raw = swap(group_raw, "tp", 1)
-    grad_logits = raw_logits * byte_valid.astype(jnp.bfloat16)
-    group_final, group_grad_hidden, grad_final, grad_mlp_low = final_grads(
-        group_raw,
-        other_raw,
-        group_bytes_valid,
-        w_head,
-        other_head,
-        w_down,
-        place_index,
-    )
-    grad_hidden = dot_plain(grad_mlp_low, w_down)
-    hidden_part = w_gate.shape[1] // members
-
-    result = from_lanes(after(result, group_grad_hidden, grad_hidden))
+    result = from_lanes(result)
     unit_normed, norm_back = jax.vjp(gated_unit, result, gate_in)
     mix_scale = mix_gain.astype(f32)
     normed_low = (unit_normed * mix_scale).reshape(patch_total, -1).astype(jnp.bfloat16)
@@ -1319,6 +1316,20 @@
     grad_result, grad_gate_in = norm_back(grad_normed * mix_scale)
     grad_z_low = grad_gate_in.reshape(patch_total, inner_width).astype(jnp.bfloat16)
     row_block = model_width // parts
+    group_raw = jnp.concatenate(
+        [raw_wide] + [after(raw, grad_normed) for raw in apart_raw], axis=0
+    )
+    other_raw = swap(group_raw, "tp", 1)
+    group_final, group_grad_hidden, unused, unused_part = final_grads(
+        group_raw,
+        other_raw,
+        group_bytes_valid,
+        w_head,
+        other_head,
+        w_down,
+        place_index,
+        members,
+    )
     dealing = after(by_lane(grad_result), bytes_all, group_halves)
     dealt = trade(dealing)
     late_sent = [
@@ -1415,13 +1426,6 @@
     )
     grad_u_part = dot_trans(grad_proj_low, w_in)
     grad_u = tp_sum(grad_u_part)
-    rest = [quarters(columns) for columns in (grad_x, grad_bc, grad_dt)]
-    rest_cols = [part.shape[-1] for part in rest]
-    rest = after(jnp.concatenate(rest, axis=-1), grad_u_part)
-    rest = jnp.pad(rest, ((0, 0), (0, 0), (0, -sum(rest_cols) % 128)))
-    rest_blocks = grad_blocks(
-        [(group_u, joined(group_swap(by_apart(rest)), grad_u_part), 0, rest.shape[-1])], 0, True
-    )
     back_global, grad_norm_global = rms_back(patch_out, gain_global, grad_u)
     grad_patch = grad_global + back_global
     side_count = parts // 2
@@ -1446,7 +1450,7 @@
         for first in range(2)
     ]
     mlp_crossed = [to_partner(mlp_far[first], 1 - first) for first in range(2)]
-    patch_taken = after(patch_taken, rest_blocks[0], *mlp_far)
+    patch_taken = after(patch_taken, *mlp_far)
     gain_side = jnp.sum(patch_taken[:, patch_total:], axis=0)
     patch_cols = patch_taken[:, :patch_total].reshape(-1, 2 * row_block)
     patch_far = patch_far_grad(patch_cols, gain_side, bytes_all)
@@ -1501,6 +1505,13 @@
     attn_high = [
         swap(attn_near[apart], "seq", QUAD * apart) for apart in range(1, parts // QUAD)
     ]
+    rest = [quarters(columns) for columns in (grad_x, grad_bc, grad_dt)]
+    rest_cols = [part.shape[-1] for part in rest]
+    rest = after(jnp.concatenate(rest, axis=-1), patch_far)
+    rest = jnp.pad(rest, ((0, 0), (0, 0), (0, -sum(rest_cols) % 128)))
+    rest_blocks = grad_blocks(
+        [(group_u, joined(group_swap(by_apart(rest)), patch_far), 0, rest.shape[-1])], 0, True
+    )
     rest_got = to_partner(after(rest_blocks[0], patch_far), 0)
     start = jnp.zeros((1,), jnp.int32)
     mlp_near = [
@@ -1515,12 +1526,12 @@
         final_attn = final_attn + after(got, *mlp_near)
     rest_far = add_side(after(rest_blocks[1], *mlp_near), rest_got, 1)
     rest_crossed = to_partner(rest_far, 1)
+    mlp_finals = [jnp.moveaxis(group_trade(part), 0, 1) for part in mlp_near]
     rest_near = near_sums(
-        [(after(rest_blocks[1], final_attn), rest_got, rest_crossed)], start
-    )
-    mlp_finals = [
-        jnp.moveaxis(group_trade(part), 0, 1) for part in mlp_near + [rest_near]
-    ]
+        [(after(rest_blocks[1], final_attn, *mlp_finals), rest_got, rest_crossed)], start
+    )
+    mlp_finals.append(jnp.moveaxis(group_trade(rest_near), 0, 1))
+
     def final_cols(final, low, count):
         return final[..., low : low + count].reshape(row_block, -1)
 

time: 672 us -> 699 us (1.040)
  starting transfers between devices: 125 us -> 164 us
  blocking collectives: 26.2 us -> 0 us
  local copies, waits for them, and re-layouts: 49.1 us -> 60.8 us
    all_to_all x1 -> x0, blocking collectives: 26.2 us -> none  [group_trade(): lax.all_to_all(blocks, 'seq', 0, 0, axis_index_groups=members, tiled=True)]
    all_to_all x5, starting transfers between devices: 26.1 us -> 50.1 us  [trade(): return lax.all_to_all(blocks, 'seq', 0, 0, tiled=True)]
    all_to_all x3 -> x4, starting transfers between devices: 12.7 us -> 29.8 us  [group_trade(): lax.all_to_all(blocks, 'seq', 0, 0, axis_index_groups=members, tiled=True)]
    all_to_all x5, waiting for transfers between devices: 26.2 us -> 17.7 us  [trade(): return lax.all_to_all(blocks, 'seq', 0, 0, tiled=True)]
    ppermute x36 -> x37, waiting for transfers between devices: 90.1 us -> 95.5 us  [swap(): lax.ppermute(block, axis, [(i, i ^ mask) for i in range(lax.axis_size(axi...]
    pallas_call x1 -> x2, Pallas kernels: 10.5 us -> 15.4 us  [final_grads(): pl.pallas_call(final_kernel, grid_spec=pltpu.PrefetchScalarGridSpec(num_s...]
    ppermute x36 -> x37, starting transfers between devices: 70.5 us -> 67.6 us  [swap(): lax.ppermute(block, axis, [(i, i ^ mask) for i in range(lax.axis_size(axi...]
    all_to_all x3 -> x4, waiting for transfers between devices: 70.1 us -> 71.6 us  [group_trade(): lax.all_to_all(blocks, 'seq', 0, 0, axis_index_groups=members, tiled=True)]
  transfers between devices with their start and end apart: 46 -> 48, of which waited for: 22 -> 18; matrix products, arithmetic and copies ran while one was open for 16% -> 17% of each run, Pallas kernels for 25% -> 25%
where the time goes in v1:
time: 699 us; the launch traced here: 687 us
  Pallas kernels  192 us (27%)
  waiting for transfers between devices  185 us (26%)
  starting transfers between devices  164 us (23%)
  local copies, waits for them, and re-layouts  60.8 us (9%)
  other arithmetic  49.2 us (7%)
  matrix products  21.5 us (3%)
  between operations  15.7 us (2%)
    ppermute x37, waiting for transfers between devices, swap(): lax.ppermute(block, axis, [(i, i ^ mask) for i in range(lax.axis_size(axi...  95.5 us
    all_to_all x4, waiting for transfers between devices, group_trade(): lax.all_to_all(blocks, 'seq', 0, 0, axis_index_groups=members, tiled=True)  71.6 us
    ppermute x37, starting transfers between devices, swap(): lax.ppermute(block, axis, [(i, i ^ mask) for i in range(lax.axis_size(axi...  67.6 us
    all_to_all x5, starting transfers between devices, trade(): return lax.all_to_all(blocks, 'seq', 0, 0, tiled=True)  50.1 us
    pallas_call x5, Pallas kernels, grad_blocks(): pl.pallas_call(partial(grad_blocks_kernel, pairs, first, relative, rows),...  37.5 us
    all_to_all x4, starting transfers between devices, group_trade(): lax.all_to_all(blocks, 'seq', 0, 0, axis_index_groups=members, tiled=True)  29.8 us
    all_to_all x5, waiting for transfers between devices, trade(): return lax.all_to_all(blocks, 'seq', 0, 0, tiled=True)  17.7 us
    pallas_call x5, Pallas kernels, add_side(): pl.pallas_call(add_kernel, grid_spec=pltpu.PrefetchScalarGridSpec(num_sca...  17.6 us
  transfers between devices with their start and end apart: 48, of which 18 were waited for; matrix products, arithmetic and copies ran while one was open for 17% of the time, Pallas kernels for 25%

profile of v1, /device:TPU:0, one launch (start us, length us, event | category | flops | bytes accessed | tf_op | source)
XLA Modules:
  0.0 687.5 jit_solution(9596755699964205674)
XLA Ops:
  7.3 9.2 %shard_map.356 = (f32[64,4096]{1,0:T(8,128)}, f32[64,1024]{1,0:T(8,128)}) custom-call(s32[1]{0:T(128)} %bitcast.core_ref, bf16[512,1024]{1,0:T(8,128)(2,1)} %bitcast.251, bf16[1024,4096]{1,0:T(8,128)(2,1)} %weight_ref.7), custom_call_target="tpu_custom_call" | custom-call | flops 1024 | bytes 1024 | tf_op jit(solution)/shard_map/pallas_call | solution.py:910
  82.6 15.5 %all-to-all-start.1 = ((f32[16,32,128]{2,1,0:T(8,128)}), f32[16,32,128]{2,1,0:T(8,128)S(1)}, u32[]{:S(2)}, u32[]{:S(2)}) async-start(f32[16,32,128]{2,1,0:T(8,128)} %bitcast.292), calls=%async_computation.1 | async-start | bytes 524288 | tf_op jit(solution)/shard_map/all_to_all | solution.py:362
  98.1 15.1 %all-to-all-done.1 = f32[16,32,128]{2,1,0:T(8,128)S(1)} async-done(((f32[16,32,128]{2,1,0:T(8,128)}), f32[16,32,128]{2,1,0:T(8,128)S(1)}, u32[]{:S(2)}, u32[]{:S(2)}) %all-to-all-start.1) | async-done | bytes 262176 | tf_op jit(solution)/shard_map/all_to_all | solution.py:362
  137.1 15.2 %shard_map.361 = (bf16[512,2048]{1,0:T(8,128)(2,1)}, bf16[512,2048]{1,0:T(8,128)(2,1)}, bf16[512,2048]{1,0:T(8,128)(2,1)}, f32[512,1024]{1,0:T(8,128)}) custom-call(bf16[512,1024]{1,0:T(8,128)(2,1)} %get-tuple-element.111.in_ref, f32[512,2048]{1,0:T(8,128)} %fusion.45.grad_ref, bf16[1024,2048]{1,0:T(8,128)(2,1)} %gate_w_ref.3, bf16[1024,2048]{1,0:T(8,128)(2,1)} %up_w_ref.3), custom_call_target="tpu_custom_call" | custom-call | flops 1024 | bytes 1024 | tf_op jit(solution)/shard_map/pallas_call | solution.py:853
  160.9 11.5 %shard_map.362 = (f32[512,1024]{1,0:T(8,128)}, bf16[512,1024]{1,0:T(8,128)(2,1)}, bf16[512,1536]{1,0:T(8,128)(2,1)}, f32[512,1024]{1,0:T(8,128)}, f32[1,1024]{1,0:T(1,128)}) custom-call(f32[512,1024]{1,0:T(8,128)} %get-tuple-element.108.x_ref, f32[512,1024]{1,0:T(8,128)} %get-tuple-element.115.final_ref, f32[512,1024]{1,0:T(8,128)} %get-tuple-element.113.own_ref, ...), custom_call_target="tpu_custom_call" | custom-call | flops 1024 | bytes 1024 | tf_op jit(solution)/shard_map/pallas_call | solution.py:749
  193.2 66.2 %all-to-all-done.2.own_ref = f32[4,512,512]{2,1,0:T(8,128)} async-done(((f32[4,512,512]{2,1,0:T(8,128)}), f32[4,512,512]{2,1,0:T(8,128)}, u32[]{:S(2)}, u32[]{:S(2)}) %all-to-all-start.2) | async-done | bytes 4194336 | tf_op jit(solution)/shard_map/all_to_all | solution.py:90
  274.9 7.9 %shard_map.364 = (f32[2,4,64,1152]{3,2,1,0:T(8,128)}, f32[2,4,64,1152]{3,2,1,0:T(8,128)}) custom-call(s32[1]{0:T(128)} %bitcast.35.member_ref, bf16[512,1024]{1,0:T(8,128)(2,1)} %get-tuple-element.121.refs_0_, bf16[512,1024]{1,0:T(8,128)(2,1)} %get-tuple-element.124.refs_1_, bf16[512,1024]{1,0:T(8,128)(2,1)} %add_convert_fusion.refs_2_, ...), custom_call_target="tpu_custom_call" | custom-call | flops 1024 | bytes 1024 | tf_op jit(solution)/shard_map/pallas_call | solution.py:201
  283.6 10.2 %shard_map.365 = (f32[512,512]{1,0:T(8,128)}, f32[8,384]{1,0:T(8,128)}, f32[8,128]{1,0:T(8,128)}) custom-call(f32[512,512]{1,0:T(8,128)} %bitcast.249, f32[512,8]{1,0:T(8,128)} %copy.147.same_ref, f32[8,384]{1,0:T(8,128)} %maximum_maximum_fusion.conv_ref, f32[8,128]{1,0:T(8,128)} %stack.87.head_ref, s32[512,1]{1,0:T(8,128)} %copy.148.seg_col, ...), custom_call_target="tpu_custom_call" | custom-call | flops 1024 | bytes 1024 | tf_op jit(solution)/shard_map/pallas_call | solution.py:548
  307.2 13.9 %collective-permute-done.9 = f32[512,128]{1,0:T(8,128)S(1)} collective-permute-done((f32[512,128]{1,0:T(8,128)}, f32[512,128]{1,0:T(8,128)S(1)}, u32[]{:S(2)}, u32[]{:S(2)}) %collective-permute-start.9) | collective-permute-done | bytes 262176 | tf_op jit(solution)/shard_map/ppermute | solution.py:65
  334.4 10.4 %shard_map.366 = (bf16[2048,1024]{1,0:T(8,128)(2,1)}, f32[2048,512]{1,0:T(8,128)}, f32[512,1024]{1,0:T(8,128)}, bf16[512,1024]{1,0:T(8,128)(2,1)}) custom-call(s32[1]{0:T(128)} %bitcast.12.member_ref.index_ref, f32[2048,128]{1,0:T(8,128)} %pad_maximum_fusion.own_ref, f32[2048,128]{1,0:T(8,128)} %collective-permute-done.11.other_ref, ...), custom_call_target="tpu_custom_call" | custom-call | flops 1024 | bytes 1024 | tf_op jit(solution)/shard_map/pallas_call | solution.py:976
  351.3 12.3 %shard_map.367 = (bf16[2048,1024]{1,0:T(8,128)(2,1)}, bf16[2048,512]{1,0:T(8,128)(2,1)}, bf16[2048,512]{1,0:T(8,128)(2,1)}, bf16[2048,512]{1,0:T(8,128)(2,1)}) custom-call(s32[2]{0:T(128)} %pad_add_fusion.place_ref, f32[4,512,512]{2,1,0:T(8,128)} %all-to-all-done.2.own_ref, f32[4,512,512]{2,1,0:T(8,128)} %collective-permute-done.12.other_ref, ...), custom_call_target="tpu_custom_call" | custom-call | flops 1024 | bytes 1024 | tf_op jit(solution)/shard_map/pallas_call | solution.py:1029
  363.7 10.9 %shard_map.368 = (f32[2,4,64,1024]{3,2,1,0:T(8,128)}, f32[2,4,64,1024]{3,2,1,0:T(8,128)}) custom-call(s32[1]{0:T(128)} %bitcast.35.member_ref, bf16[2048,1024]{1,0:T(8,128)(2,1)} %get-tuple-element.132.refs_0_, bf16[2048,1024]{1,0:T(8,128)(2,1)} %get-tuple-element.135.refs_1_.refs_0_, bf16[2048,512]{1,0:T(8,128)(2,1)} %get-tuple-element.136.refs_2_, ...), custom_call_target="tpu_custom_call" | custom-call | flops 1024 | bytes 1024 | tf_op jit(solution)/shard_map/pallas_call | solution.py:201
  390.3 8.3 %collective-permute-done.15 = f32[64,1280]{1,0:T(8,128)S(1)} collective-permute-done((f32[64,1280]{1,0:T(8,128)S(1)}, f32[64,1280]{1,0:T(8,128)S(1)}, u32[]{:S(2)}, u32[]{:S(2)}) %collective-permute-start.15) | collective-permute-done | bytes 327712 | tf_op jit(solution)/shard_map/ppermute | solution.py:65
  409.0 9.0 %shard_map.371 = (f32[2,4,64,1024]{3,2,1,0:T(8,128)}, f32[2,4,64,1024]{3,2,1,0:T(8,128)}) custom-call(s32[1]{0:T(128)} %bitcast.35.member_ref, bf16[2048,1024]{1,0:T(8,128)(2,1)} %get-tuple-element.135.refs_1_.refs_0_, bf16[256,1024]{1,0:T(8,128)(2,1)} %fusion.1.refs_1_, bf16[256,1024]{1,0:T(8,128)(2,1)} %fusion.refs_2_.refs_0_, ...), custom_call_target="tpu_custom_call" | custom-call | flops 1024 | bytes 1024 | tf_op jit(solution)/shard_map/pallas_call | solution.py:201
  433.9 16.3 %all-to-all-start.5 = ((f32[8,72,128]{2,1,0:T(8,128)}), f32[8,72,128]{2,1,0:T(8,128)S(1)}, u32[]{:S(2)}, u32[]{:S(2)}) async-start(f32[8,72,128]{2,1,0:T(8,128)} %pad_maximum_fusion.12), calls=%async_computation.5 | async-start | bytes 589824 | tf_op jit(solution)/shard_map/all_to_all | solution.py:1444
  450.9 17.5 %collective-permute-done.22.refs_1_ = f32[2,4,64,1024]{3,2,1,0:T(8,128)} collective-permute-done((f32[2,4,64,1024]{3,2,1,0:T(8,128)}, f32[2,4,64,1024]{3,2,1,0:T(8,128)}, u32[]{:S(2)}, u32[]{:S(2)}) %collective-permute-start.22) | collective-permute-done | bytes 2097184 | tf_op jit(solution)/shard_map/ppermute | solution.py:65
  489.2 17.4 %all-to-all-start.9 = ((f32[16,40,128]{2,1,0:T(8,128)}), f32[16,40,128]{2,1,0:T(8,128)S(1)}, u32[]{:S(2)}, u32[]{:S(2)}) async-start(f32[16,40,128]{2,1,0:T(8,128)} %broadcast_in_dim.73), calls=%async_computation.9 | async-start | bytes 655360 | tf_op jit(solution)/shard_map/all_to_all | solution.py:362
  506.6 8.2 %collective-permute-done.25.refs_2_ = f32[4,64,1024]{2,1,0:T(8,128)} collective-permute-done((f32[4,64,1024]{2,1,0:T(8,128)}, f32[4,64,1024]{2,1,0:T(8,128)}, u32[]{:S(2)}, u32[]{:S(2)}) %collective-permute-start.25) | collective-permute-done | bytes 1048608 | tf_op jit(solution)/shard_map/ppermute | solution.py:65
  520.1 13.4 %collective-permute-done.32.refs_2_ = f32[4,64,1024]{2,1,0:T(8,128)S(1)} collective-permute-done((f32[4,64,1024]{2,1,0:T(8,128)}, f32[4,64,1024]{2,1,0:T(8,128)S(1)}, u32[]{:S(2)}, u32[]{:S(2)}) %collective-permute-start.32) | collective-permute-done | bytes 1048608 | tf_op jit(solution)/shard_map/ppermute | solution.py:65
  538.3 16.7 %all-to-all-start.7 = ((f32[4,64,1024]{2,1,0:T(8,128)}), f32[4,64,1024]{2,1,0:T(8,128)S(1)}, u32[]{:S(2)}, u32[]{:S(2)}) async-start(f32[4,64,1024]{2,1,0:T(8,128)} %shard_map.380), calls=%async_computation.7 | async-start | bytes 2097152 | tf_op jit(solution)/shard_map/all_to_all | solution.py:90
  569.4 10.4 %collective-permute-done.30 = f32[64,384]{1,0:T(8,128)S(1)} collective-permute-done((f32[64,384]{1,0:T(8,128)S(1)}, f32[64,384]{1,0:T(8,128)S(1)}, u32[]{:S(2)}, u32[]{:S(2)}) %collective-permute-start.30) | collective-permute-done | bytes 98336 | tf_op jit(solution)/shard_map/ppermute | solution.py:65
  579.8 25.0 %collective-permute-start.33 = (f32[64,2176]{1,0:T(8,128)}, f32[64,2176]{1,0:T(8,128)}, u32[]{:S(2)}, u32[]{:S(2)}) collective-permute-start(f32[64,2176]{1,0:T(8,128)} %get-tuple-element.205), channel_id=1, source_target_pairs={{0,16},{2,18},{4,20},{6,22},{8,24},{10,26},{12,28},{14,30},{16,0},... | collective-permute-start | bytes 1671176 | tf_op jit(solution)/shard_map/ppermute | solution.py:65
  606.6 12.4 %shard_map.375 = f32[512,512]{1,0:T(8,128)} custom-call(s32[1]{0:T(128)} %bitcast.core_ref, f32[64,1024]{1,0:T(8,128)} %copy-done.17, bf16[1024,4096]{1,0:T(8,128)(2,1)} %weight_ref.7, f32[512,1024]{1,0:T(8,128)} %get-tuple-element.196.stream_ref), custom_call_target="tpu_custom_call" | custom-call | flops 1024 | bytes 1024 | tf_op jit(solution)/shard_map/pallas_call | solution.py:1076
  649.9 9.1 %shard_map.376 = f32[64,4096]{1,0:T(8,128)} custom-call(f32[512,128]{1,0:T(8,128)} %bitcast.262, f32[512,4096]{1,0:T(8,128)} %all-gather.2.cloned.1.call-done.bytes_ref.refs_0_.refs_1_.refs_2_.refs_3_.refs_4_.refs_5_.refs_6_.refs_7_, f32[512,4096]{1,0:T(8,128)} %all-gather.2.cloned.1.call-done.bytes_ref.refs_0_.refs_1_.refs_2_.refs_3_.refs_4_.refs_5_.refs_6_.refs_7_, ...), custom_call_target="tpu_custom_call" | custom-call | flops 1024 | bytes 1024 | tf_op jit(solution)/shard_map/pallas_call | solution.py:347
  (427 shorter events, 309.7 us)
Async XLA Ops:
  7.2 252.1 %all-gather.2.cloned.1.call-start = ((), (), s32[]{:S(2)}) async-start(), calls=%async_computation.10 | async-start | bytes 9437184 | tf_op jit(solution)/shard_map/all_gather | solution.py:1215
  17.8 43.9 %collective-permute-start.1 = (f32[512,128]{1,0:T(8,128)}, f32[512,128]{1,0:T(8,128)}, u32[]{:S(2)}, u32[]{:S(2)}) collective-permute-start(f32[512,128]{1,0:T(8,128)} %bitcast_convert_fusion.own_ref), channel_id=1, source_target_pairs={{0,1},{1,0},{2,3},{3,2},{4,5},{5,4},{6,7},{7,6},{8,9},{9,8},{10,11... | collective-permute-start | bytes 786440 | tf_op jit(solution)/shard_map/ppermute | solution.py:65
  27.2 47.7 %all-to-all-start = ((f32[16,32,512]{2,1,0:T(8,128)}), f32[16,32,512]{2,1,0:T(8,128)S(1)}, u32[]{:S(2)}, u32[]{:S(2)}) async-start(f32[16,32,512]{2,1,0:T(8,128)} %select_maximum_fusion), calls=%async_computation | async-start | bytes 2097152 | tf_op jit(solution)/shard_map/all_to_all | solution.py:362
  155.1 104.2 %all-to-all-start.2 = ((f32[4,512,512]{2,1,0:T(8,128)}), f32[4,512,512]{2,1,0:T(8,128)}, u32[]{:S(2)}, u32[]{:S(2)}) async-start(f32[4,512,512]{2,1,0:T(8,128)} %broadcast_in_dim.33), calls=%async_computation.2 | async-start | bytes 8388608 | tf_op jit(solution)/shard_map/all_to_all | solution.py:90
  181.1 84.4 %collective-permute-start.5 = (f32[512,1024]{1,0:T(8,128)}, f32[512,1024]{1,0:T(8,128)}, u32[]{:S(2)}, u32[]{:S(2)}) collective-permute-start(f32[512,1024]{1,0:T(8,128)} %fusion.47), channel_id=1, source_target_pairs={{0,1},{1,0},{2,3},{3,2},{4,5},{5,4},{6,7},{7,6},{8,9},{9,8},{10,11... | collective-permute-start | bytes 6291464 | tf_op jit(solution)/shard_map/ppermute | solution.py:65
  293.8 55.5 %collective-permute-start.12 = (f32[4,512,512]{2,1,0:T(8,128)}, f32[4,512,512]{2,1,0:T(8,128)}, u32[]{:S(2)}, u32[]{:S(2)}) collective-permute-start(f32[4,512,512]{2,1,0:T(8,128)} %all-to-all-done.2.own_ref), channel_id=1, source_target_pairs={{0,1},{1,0},{2,3},{3,2},{4,5},{5,4},{6,7},{7,6},{8,9},{9,8},{10,11... | collective-permute-start | bytes 12582920 | tf_op jit(solution)/shard_map/ppermute | solution.py:65
  297.8 79.4 %collective-permute-start.19 = (f32[2,4,64,1024]{3,2,1,0:T(8,128)}, f32[2,4,64,1024]{3,2,1,0:T(8,128)S(1)}, u32[]{:S(2)}, u32[]{:S(2)}) collective-permute-start(f32[2,4,64,1024]{3,2,1,0:T(8,128)} %get-tuple-element.123), channel_id=1, source_target_pairs={{0,2},{2,0},{4,6},{6,4},{8,10},{10,8},{12,14},{14,12},{16,18},{18,... | collective-permute-start | bytes 6291464 | tf_op jit(solution)/shard_map/ppermute | solution.py:65
  305.3 81.3 %collective-permute-start.20 = (f32[2,4,64,1152]{3,2,1,0:T(8,128)}, f32[2,4,64,1152]{3,2,1,0:T(8,128)}, u32[]{:S(2)}, u32[]{:S(2)}) collective-permute-start(f32[2,4,64,1152]{3,2,1,0:T(8,128)} %get-tuple-element.126), channel_id=1, source_target_pairs={{0,4},{2,6},{4,0},{6,2},{8,12},{10,14},{12,8},{14,10},{16,20},{18,... | collective-permute-start | bytes 7077896 | tf_op jit(solution)/shard_map/ppermute | solution.py:65
  329.9 44.6 %collective-permute-start.13 = (f32[64,1280]{1,0:T(8,128)}, f32[64,1280]{1,0:T(8,128)}, u32[]{:S(2)}, u32[]{:S(2)}) collective-permute-start(f32[64,1280]{1,0:T(8,128)} %get-tuple-element.227), channel_id=1, source_target_pairs={{0,8},{2,10},{4,12},{6,14},{8,0},{10,2},{12,4},{14,6},{16,24},{18,... | collective-permute-start | bytes 983048 | tf_op jit(solution)/shard_map/ppermute | solution.py:65
  330.2 46.8 %collective-permute-start.14 = (f32[64,1280]{1,0:T(8,128)}, f32[64,1280]{1,0:T(8,128)}, u32[]{:S(2)}, u32[]{:S(2)}) collective-permute-start(f32[64,1280]{1,0:T(8,128)} %get-tuple-element.228), channel_id=1, source_target_pairs={{0,16},{2,18},{4,20},{6,22},{8,24},{10,26},{12,28},{14,30},{16,0},... | collective-permute-start | bytes 983048 | tf_op jit(solution)/shard_map/ppermute | solution.py:65
  344.7 73.3 %all-to-all-start.4 = ((f32[16,32,512]{2,1,0:T(8,128)}), f32[16,32,512]{2,1,0:T(8,128)S(1)}, u32[]{:S(2)}, u32[]{:S(2)}) async-start(f32[16,32,512]{2,1,0:T(8,128)} %bitcast.283), calls=%async_computation.4 | async-start | bytes 2097152 | tf_op jit(solution)/shard_map/all_to_all | solution.py:362
  349.3 49.3 %collective-permute-start.16 = (f32[64,1280]{1,0:T(8,128)}, f32[64,1280]{1,0:T(8,128)S(1)}, u32[]{:S(2)}, u32[]{:S(2)}) collective-permute-start(f32[64,1280]{1,0:T(8,128)} %get-tuple-element.219), channel_id=1, source_target_pairs={{0,8},{2,10},{4,12},{6,14},{8,0},{10,2},{12,4},{14,6},{16,24},{18,... | collective-permute-start | bytes 983048 | tf_op jit(solution)/shard_map/ppermute | solution.py:65
  419.5 48.9 %collective-permute-start.22 = (f32[2,4,64,1024]{3,2,1,0:T(8,128)}, f32[2,4,64,1024]{3,2,1,0:T(8,128)}, u32[]{:S(2)}, u32[]{:S(2)}) collective-permute-start(f32[2,4,64,1024]{3,2,1,0:T(8,128)} %get-tuple-element.138), channel_id=1, source_target_pairs={{0,2},{2,0},{4,6},{6,4},{8,10},{10,8},{12,14},{14,12},{16,18},{18,... | collective-permute-start | bytes 6291464 | tf_op jit(solution)/shard_map/ppermute | solution.py:65
  421.0 51.0 %collective-permute-start.23 = (f32[2,4,64,1024]{3,2,1,0:T(8,128)}, f32[2,4,64,1024]{3,2,1,0:T(8,128)S(1)}, u32[]{:S(2)}, u32[]{:S(2)}) collective-permute-start(f32[2,4,64,1024]{3,2,1,0:T(8,128)} %get-tuple-element.153), channel_id=1, source_target_pairs={{0,4},{2,6},{4,0},{6,2},{8,12},{10,14},{12,8},{14,10},{16,20},{18,... | collective-permute-start | bytes 6291464 | tf_op jit(solution)/shard_map/ppermute | solution.py:65
  433.9 43.0 %all-to-all-start.5 = ((f32[8,72,128]{2,1,0:T(8,128)}), f32[8,72,128]{2,1,0:T(8,128)S(1)}, u32[]{:S(2)}, u32[]{:S(2)}) async-start(f32[8,72,128]{2,1,0:T(8,128)} %pad_maximum_fusion.12), calls=%async_computation.5 | async-start | bytes 589824 | tf_op jit(solution)/shard_map/all_to_all | solution.py:1444
  450.2 64.6 %collective-permute-start.26 = (f32[4,64,1152]{2,1,0:T(8,128)}, f32[4,64,1152]{2,1,0:T(8,128)}, u32[]{:S(2)}, u32[]{:S(2)}) collective-permute-start(f32[4,64,1152]{2,1,0:T(8,128)} %shard_map.370), channel_id=1, source_target_pairs={{0,2},{2,0},{4,6},{6,4},{8,10},{10,8},{12,14},{14,12},{16,18},{18,... | collective-permute-start | bytes 3538952 | tf_op jit(solution)/shard_map/ppermute | solution.py:65
  487.9 45.7 %collective-permute-start.32 = (f32[4,64,1024]{2,1,0:T(8,128)}, f32[4,64,1024]{2,1,0:T(8,128)S(1)}, u32[]{:S(2)}, u32[]{:S(2)}) collective-permute-start(f32[4,64,1024]{2,1,0:T(8,128)} %shard_map.372), channel_id=1, source_target_pairs={{0,4},{2,6},{4,0},{6,2},{8,12},{10,14},{12,8},{14,10},{16,20},{18,... | collective-permute-start | bytes 3145736 | tf_op jit(solution)/shard_map/ppermute | solution.py:65
  489.2 49.1 %all-to-all-start.9 = ((f32[16,40,128]{2,1,0:T(8,128)}), f32[16,40,128]{2,1,0:T(8,128)S(1)}, u32[]{:S(2)}, u32[]{:S(2)}) async-start(f32[16,40,128]{2,1,0:T(8,128)} %broadcast_in_dim.73), calls=%async_computation.9 | async-start | bytes 655360 | tf_op jit(solution)/shard_map/all_to_all | solution.py:362
  538.3 90.9 %all-to-all-start.7 = ((f32[4,64,1024]{2,1,0:T(8,128)}), f32[4,64,1024]{2,1,0:T(8,128)S(1)}, u32[]{:S(2)}, u32[]{:S(2)}) async-start(f32[4,64,1024]{2,1,0:T(8,128)} %shard_map.380), calls=%async_computation.7 | async-start | bytes 2097152 | tf_op jit(solution)/shard_map/all_to_all | solution.py:90
  557.2 67.2 %collective-permute-start.27 = (f32[4,64,1024]{2,1,0:T(8,128)}, f32[4,64,1024]{2,1,0:T(8,128)S(1)}, u32[]{:S(2)}, u32[]{:S(2)}) collective-permute-start(f32[4,64,1024]{2,1,0:T(8,128)} %shard_map.373), channel_id=1, source_target_pairs={{0,2},{2,0},{4,6},{6,4},{8,10},{10,8},{12,14},{14,12},{16,18},{18,... | collective-permute-start | bytes 3145736 | tf_op jit(solution)/shard_map/ppermute | solution.py:65
  562.2 43.6 %collective-permute-start.29 = (f32[64,384]{1,0:T(8,128)S(1)}, f32[64,384]{1,0:T(8,128)S(1)}, u32[]{:S(2)}, u32[]{:S(2)}) collective-permute-start(f32[64,384]{1,0:T(8,128)S(1)} %bitcast.316), channel_id=1, source_target_pairs={{0,16},{2,18},{4,20},{6,22},{8,24},{10,26},{12,28},{14,30},{16,0},... | collective-permute-start | bytes 294920 | tf_op jit(solution)/shard_map/ppermute | solution.py:65
  562.3 43.5 %collective-permute-start.28 = (f32[64,384]{1,0:T(8,128)S(1)}, f32[64,384]{1,0:T(8,128)S(1)}, u32[]{:S(2)}, u32[]{:S(2)}) collective-permute-start(f32[64,384]{1,0:T(8,128)S(1)} %bitcast.315), channel_id=1, source_target_pairs={{0,8},{2,10},{4,12},{6,14},{8,0},{10,2},{12,4},{14,6},{16,24},{18,... | collective-permute-start | bytes 294920 | tf_op jit(solution)/shard_map/ppermute | solution.py:65
  565.6 74.7 %collective-permute-start.34 = (f32[64,2176]{1,0:T(8,128)}, f32[64,2176]{1,0:T(8,128)}, u32[]{:S(2)}, u32[]{:S(2)}) collective-permute-start(f32[64,2176]{1,0:T(8,128)} %get-tuple-element.204), channel_id=1, source_target_pairs={{0,24},{2,26},{4,28},{6,30},{8,16},{10,18},{12,20},{14,22},{16,8},... | collective-permute-start | bytes 1671176 | tf_op jit(solution)/shard_map/ppermute | solution.py:65
  579.8 64.4 %collective-permute-start.33 = (f32[64,2176]{1,0:T(8,128)}, f32[64,2176]{1,0:T(8,128)}, u32[]{:S(2)}, u32[]{:S(2)}) collective-permute-start(f32[64,2176]{1,0:T(8,128)} %get-tuple-element.205), channel_id=1, source_target_pairs={{0,16},{2,18},{4,20},{6,22},{8,24},{10,26},{12,28},{14,30},{16,0},... | collective-permute-start | bytes 1671176 | tf_op jit(solution)/shard_map/ppermute | solution.py:65
  (90 other events, 1495.6 us)
Sparse Core Ops, SparseCore 0:
  16.7 178.1 all-gather.1

commit v2 on v1

--- a/solution.py
+++ b/solution.py
@@ -1330,7 +1330,7 @@
         place_index,
         members,
     )
-    dealing = after(by_lane(grad_result), bytes_all, group_halves)
+    dealing = after(by_lane(grad_result), bytes_all, group_grad_hidden, group_halves)
     dealt = trade(dealing)
     late_sent = [
         jnp.concatenate([grad_global, part], axis=-1) for part in by_apart(quarters(grad_gate_in))
@@ -1426,6 +1426,13 @@
     )
     grad_u_part = dot_trans(grad_proj_low, w_in)
     grad_u = tp_sum(grad_u_part)
+    rest = [quarters(columns) for columns in (grad_x, grad_bc, grad_dt)]
+    rest_cols = [part.shape[-1] for part in rest]
+    rest = after(jnp.concatenate(rest, axis=-1), grad_u_part)
+    rest = jnp.pad(rest, ((0, 0), (0, 0), (0, -sum(rest_cols) % 128)))
+    rest_blocks = grad_blocks(
+        [(group_u, joined(group_swap(by_apart(rest)), grad_u_part), 0, rest.shape[-1])], 0, True
+    )
     back_global, grad_norm_global = rms_back(patch_out, gain_global, grad_u)
     grad_patch = grad_global + back_global
     side_count = parts // 2
@@ -1450,7 +1457,7 @@
         for first in range(2)
     ]
     mlp_crossed = [to_partner(mlp_far[first], 1 - first) for first in range(2)]
-    patch_taken = after(patch_taken, *mlp_far)
+    patch_taken = after(patch_taken, rest_blocks[0], *mlp_far)
     gain_side = jnp.sum(patch_taken[:, patch_total:], axis=0)
     patch_cols = patch_taken[:, :patch_total].reshape(-1, 2 * row_block)
     patch_far = patch_far_grad(patch_cols, gain_side, bytes_all)
@@ -1505,13 +1512,6 @@
     attn_high = [
         swap(attn_near[apart], "seq", QUAD * apart) for apart in range(1, parts // QUAD)
     ]
-    rest = [quarters(columns) for columns in (grad_x, grad_bc, grad_dt)]
-    rest_cols = [part.shape[-1] for part in rest]
-    rest = after(jnp.concatenate(rest, axis=-1), patch_far)
-    rest = jnp.pad(rest, ((0, 0), (0, 0), (0, -sum(rest_cols) % 128)))
-    rest_blocks = grad_blocks(
-        [(group_u, joined(group_swap(by_apart(rest)), patch_far), 0, rest.shape[-1])], 0, True
-    )
     rest_got = to_partner(after(rest_blocks[0], patch_far), 0)
     start = jnp.zeros((1,), jnp.int32)
     mlp_near = [

time: 699 us -> 695 us (level)
  starting transfers between devices: 164 us -> 113 us
  waiting for transfers between devices: 185 us -> 232 us
    ppermute x37, waiting for transfers between devices: 95.5 us -> 191 us  [swap(): lax.ppermute(block, axis, [(i, i ^ mask) for i in range(lax.axis_size(axi...]
    all_to_all x4, waiting for transfers between devices: 71.6 us -> 23.1 us  [group_trade(): lax.all_to_all(blocks, 'seq', 0, 0, axis_index_groups=members, tiled=True)]
    ppermute x37, starting transfers between devices: 67.6 us -> 39.5 us  [swap(): lax.ppermute(block, axis, [(i, i ^ mask) for i in range(lax.axis_size(axi...]
    all_to_all x5, starting transfers between devices: 50.1 us -> 37.8 us  [trade(): return lax.all_to_all(blocks, 'seq', 0, 0, tiled=True)]
    all_to_all x4, starting transfers between devices: 29.8 us -> 18.8 us  [group_trade(): lax.all_to_all(blocks, 'seq', 0, 0, axis_index_groups=members, tiled=True)]
  transfers between devices with their start and end apart: 48 -> 48, of which waited for: 18 -> 18; matrix products, arithmetic and copies ran while one was open for 17% -> 18% of each run, Pallas kernels for 25% -> 25%
where the time goes in v2:
time: 695 us; the launch traced here: 683 us
  waiting for transfers between devices  232 us (33%)
  Pallas kernels  192 us (28%)
  starting transfers between devices  113 us (16%)
  local copies, waits for them, and re-layouts  64 us (9%)
  other arithmetic  44.6 us (6%)
  matrix products  22.3 us (3%)
  between operations  15.7 us (2%)
    ppermute x37, waiting for transfers between devices, swap(): lax.ppermute(block, axis, [(i, i ^ mask) for i in range(lax.axis_size(axi...  191 us
    ppermute x37, starting transfers between devices, swap(): lax.ppermute(block, axis, [(i, i ^ mask) for i in range(lax.axis_size(axi...  39.5 us
    all_to_all x5, starting transfers between devices, trade(): return lax.all_to_all(blocks, 'seq', 0, 0, tiled=True)  37.8 us
    pallas_call x5, Pallas kernels, grad_blocks(): pl.pallas_call(partial(grad_blocks_kernel, pairs, first, relative, rows),...  37.4 us
    all_to_all x4, waiting for transfers between devices, group_trade(): lax.all_to_all(blocks, 'seq', 0, 0, axis_index_groups=members, tiled=True)  23.1 us
    all_to_all x4, starting transfers between devices, group_trade(): lax.all_to_all(blocks, 'seq', 0, 0, axis_index_groups=members, tiled=True)  18.8 us
    all_to_all x5, waiting for transfers between devices, trade(): return lax.all_to_all(blocks, 'seq', 0, 0, tiled=True)  17.8 us
    pallas_call x5, Pallas kernels, add_side(): pl.pallas_call(add_kernel, grid_spec=pltpu.PrefetchScalarGridSpec(num_sca...  17.6 us
  transfers between devices with their start and end apart: 48, of which 18 were waited for; matrix products, arithmetic and copies ran while one was open for 18% of the time, Pallas kernels for 25%

profile of v2, /device:TPU:0, one launch (start us, length us, event | category | flops | bytes accessed | tf_op | source)
XLA Modules:
  0.0 683.2 jit_solution(9436883221801276286)
XLA Ops:
  7.3 9.2 %shard_map.356 = (f32[64,4096]{1,0:T(8,128)}, f32[64,1024]{1,0:T(8,128)}) custom-call(s32[1]{0:T(128)} %bitcast.core_ref, bf16[512,1024]{1,0:T(8,128)(2,1)} %bitcast.251, bf16[1024,4096]{1,0:T(8,128)(2,1)} %weight_ref.7), custom_call_target="tpu_custom_call" | custom-call | flops 1024 | bytes 1024 | tf_op jit(solution)/shard_map/pallas_call | solution.py:910
  26.4 7.9 %all-to-all-start = ((f32[16,32,512]{2,1,0:T(8,128)}), f32[16,32,512]{2,1,0:T(8,128)S(1)}, u32[]{:S(2)}, u32[]{:S(2)}) async-start(f32[16,32,512]{2,1,0:T(8,128)} %select_maximum_fusion), calls=%async_computation | async-start | bytes 2097152 | tf_op jit(solution)/shard_map/all_to_all | solution.py:362
  81.7 16.2 %all-to-all-start.1 = ((f32[16,32,128]{2,1,0:T(8,128)}), f32[16,32,128]{2,1,0:T(8,128)S(1)}, u32[]{:S(2)}, u32[]{:S(2)}) async-start(f32[16,32,128]{2,1,0:T(8,128)} %bitcast.292), calls=%async_computation.1 | async-start | bytes 524288 | tf_op jit(solution)/shard_map/all_to_all | solution.py:362
  98.0 15.3 %all-to-all-done.1 = f32[16,32,128]{2,1,0:T(8,128)S(1)} async-done(((f32[16,32,128]{2,1,0:T(8,128)}), f32[16,32,128]{2,1,0:T(8,128)S(1)}, u32[]{:S(2)}, u32[]{:S(2)}) %all-to-all-start.1) | async-done | bytes 262176 | tf_op jit(solution)/shard_map/all_to_all | solution.py:362
  118.3 7.8 %shard_map.359 = (f32[512,1024]{1,0:T(8,128)}, bf16[512,1024]{1,0:T(8,128)(2,1)}, bf16[512,1536]{1,0:T(8,128)(2,1)}, bf16[512,512]{1,0:T(8,128)(2,1)}, f32[512,1024]{1,0:T(8,128)}) custom-call(bf16[512,1024]{1,0:T(8,128)(2,1)} %bitcast.252, f32[64,1024]{1,0:T(8,128)} %multiply_add_fusion.patch_ref, f32[1,1024]{1,0:T(1,128)} %bitcast.321, ...), custom_call_target="tpu_custom_call" | custom-call | flops 1024 | bytes 1024 | tf_op jit(solution)/shard_map/pallas_call | solution.py:645
  137.1 15.3 %shard_map.361 = (bf16[512,2048]{1,0:T(8,128)(2,1)}, bf16[512,2048]{1,0:T(8,128)(2,1)}, bf16[512,2048]{1,0:T(8,128)(2,1)}, f32[512,1024]{1,0:T(8,128)}) custom-call(bf16[512,1024]{1,0:T(8,128)(2,1)} %get-tuple-element.111.in_ref, f32[512,2048]{1,0:T(8,128)} %fusion.45.grad_ref, bf16[1024,2048]{1,0:T(8,128)(2,1)} %gate_w_ref.3, bf16[1024,2048]{1,0:T(8,128)(2,1)} %up_w_ref.3), custom_call_target="tpu_custom_call" | custom-call | flops 1024 | bytes 1024 | tf_op jit(solution)/shard_map/pallas_call | solution.py:853
  161.0 11.6 %shard_map.362 = (f32[512,1024]{1,0:T(8,128)}, bf16[512,1024]{1,0:T(8,128)(2,1)}, bf16[512,1536]{1,0:T(8,128)(2,1)}, f32[512,1024]{1,0:T(8,128)}, f32[1,1024]{1,0:T(1,128)}) custom-call(f32[512,1024]{1,0:T(8,128)} %get-tuple-element.108.x_ref, f32[512,1024]{1,0:T(8,128)} %get-tuple-element.115.final_ref, f32[512,1024]{1,0:T(8,128)} %get-tuple-element.113.own_ref, ...), custom_call_target="tpu_custom_call" | custom-call | flops 1024 | bytes 1024 | tf_op jit(solution)/shard_map/pallas_call | solution.py:749
  189.0 54.3 %collective-permute-done.10 = f32[512,128]{1,0:T(8,128)S(1)} collective-permute-done((f32[512,128]{1,0:T(8,128)}, f32[512,128]{1,0:T(8,128)S(1)}, u32[]{:S(2)}, u32[]{:S(2)}) %collective-permute-start.10) | collective-permute-done | bytes 262176 | tf_op jit(solution)/shard_map/ppermute | solution.py:65
  243.4 38.5 %collective-permute-done.9 = f32[512,128]{1,0:T(8,128)S(1)} collective-permute-done((f32[512,128]{1,0:T(8,128)}, f32[512,128]{1,0:T(8,128)S(1)}, u32[]{:S(2)}, u32[]{:S(2)}) %collective-permute-start.9) | collective-permute-done | bytes 262176 | tf_op jit(solution)/shard_map/ppermute | solution.py:65
  288.3 10.3 %shard_map.363 = (bf16[2048,1024]{1,0:T(8,128)(2,1)}, f32[2048,512]{1,0:T(8,128)}, f32[512,1024]{1,0:T(8,128)}, bf16[512,1024]{1,0:T(8,128)(2,1)}) custom-call(s32[1]{0:T(128)} %bitcast.12.member_ref.index_ref, f32[2048,128]{1,0:T(8,128)} %copy-done.15, f32[2048,128]{1,0:T(8,128)} %collective-permute-done.11.other_ref, f32[2048,1]{1,0:T(8,128)} %broadcast_in_dim.75.mask_ref, ...), custom_call_target="tpu_custom_call" | custom-call | flops 1024 | bytes 1024 | tf_op jit(solution)/shard_map/pallas_call | solution.py:976
  313.4 7.9 %shard_map.365 = (f32[2,4,64,1152]{3,2,1,0:T(8,128)}, f32[2,4,64,1152]{3,2,1,0:T(8,128)}) custom-call(s32[1]{0:T(128)} %bitcast.39.member_ref, bf16[512,1024]{1,0:T(8,128)(2,1)} %get-tuple-element.125.refs_0_, bf16[512,1024]{1,0:T(8,128)(2,1)} %get-tuple-element.128.refs_1_, bf16[512,1024]{1,0:T(8,128)(2,1)} %add_convert_fusion.refs_2_, ...), custom_call_target="tpu_custom_call" | custom-call | flops 1024 | bytes 1024 | tf_op jit(solution)/shard_map/pallas_call | solution.py:201
  322.1 10.2 %shard_map.366 = (f32[512,512]{1,0:T(8,128)}, f32[8,384]{1,0:T(8,128)}, f32[8,128]{1,0:T(8,128)}) custom-call(f32[512,512]{1,0:T(8,128)} %bitcast.249, f32[512,8]{1,0:T(8,128)} %copy.147.same_ref, f32[8,384]{1,0:T(8,128)} %maximum_maximum_fusion.conv_ref, f32[8,128]{1,0:T(8,128)} %stack.87.head_ref, s32[512,1]{1,0:T(8,128)} %copy.148.seg_col, ...), custom_call_target="tpu_custom_call" | custom-call | flops 1024 | bytes 1024 | tf_op jit(solution)/shard_map/pallas_call | solution.py:548
  352.2 12.4 %shard_map.367 = (bf16[2048,1024]{1,0:T(8,128)(2,1)}, bf16[2048,512]{1,0:T(8,128)(2,1)}, bf16[2048,512]{1,0:T(8,128)(2,1)}, bf16[2048,512]{1,0:T(8,128)(2,1)}) custom-call(s32[2]{0:T(128)} %pad_add_fusion.place_ref, f32[4,512,512]{2,1,0:T(8,128)} %all-to-all-done.2.own_ref, f32[4,512,512]{2,1,0:T(8,128)} %collective-permute-done.12.other_ref, ...), custom_call_target="tpu_custom_call" | custom-call | flops 1024 | bytes 1024 | tf_op jit(solution)/shard_map/pallas_call | solution.py:1029
  364.6 10.9 %shard_map.368 = (f32[2,4,64,1024]{3,2,1,0:T(8,128)}, f32[2,4,64,1024]{3,2,1,0:T(8,128)}) custom-call(s32[1]{0:T(128)} %bitcast.39.member_ref, bf16[2048,1024]{1,0:T(8,128)(2,1)} %get-tuple-element.133.refs_0_, bf16[2048,1024]{1,0:T(8,128)(2,1)} %get-tuple-element.135.refs_1_.refs_0_, bf16[2048,512]{1,0:T(8,128)(2,1)} %get-tuple-element.136.refs_2_, ...), custom_call_target="tpu_custom_call" | custom-call | flops 1024 | bytes 1024 | tf_op jit(solution)/shard_map/pallas_call | solution.py:201
  378.3 11.3 %collective-permute-done.19.refs_1_ = f32[2,4,64,1024]{3,2,1,0:T(8,128)S(1)} collective-permute-done((f32[2,4,64,1024]{3,2,1,0:T(8,128)}, f32[2,4,64,1024]{3,2,1,0:T(8,128)S(1)}, u32[]{:S(2)}, u32[]{:S(2)}) %collective-permute-start.19) | collective-permute-done | bytes 2097184 | tf_op jit(solution)/shard_map/ppermute | solution.py:65
  404.7 7.1 %collective-permute-done.17 = f32[64,1280]{1,0:T(8,128)S(1)} collective-permute-done((f32[64,1280]{1,0:T(8,128)S(1)}, f32[64,1280]{1,0:T(8,128)S(1)}, u32[]{:S(2)}, u32[]{:S(2)}) %collective-permute-start.17) | collective-permute-done | bytes 327712 | tf_op jit(solution)/shard_map/ppermute | solution.py:65
  415.2 9.0 %shard_map.371 = (f32[2,4,64,1024]{3,2,1,0:T(8,128)}, f32[2,4,64,1024]{3,2,1,0:T(8,128)}) custom-call(s32[1]{0:T(128)} %bitcast.39.member_ref, bf16[2048,1024]{1,0:T(8,128)(2,1)} %get-tuple-element.135.refs_1_.refs_0_, bf16[256,1024]{1,0:T(8,128)(2,1)} %fusion.1.refs_1_, bf16[256,1024]{1,0:T(8,128)(2,1)} %fusion.refs_2_.refs_0_, ...), custom_call_target="tpu_custom_call" | custom-call | flops 1024 | bytes 1024 | tf_op jit(solution)/shard_map/pallas_call | solution.py:201
  439.6 17.1 %all-to-all-start.5 = ((f32[8,72,128]{2,1,0:T(8,128)}), f32[8,72,128]{2,1,0:T(8,128)S(1)}, u32[]{:S(2)}, u32[]{:S(2)}) async-start(f32[8,72,128]{2,1,0:T(8,128)} %pad_maximum_fusion.12), calls=%async_computation.5 | async-start | bytes 589824 | tf_op jit(solution)/shard_map/all_to_all | solution.py:1451
  508.8 18.9 %collective-permute-done.28.refs_2_ = f32[4,64,1024]{2,1,0:T(8,128)} collective-permute-done((f32[4,64,1024]{2,1,0:T(8,128)}, f32[4,64,1024]{2,1,0:T(8,128)}, u32[]{:S(2)}, u32[]{:S(2)}) %collective-permute-start.28) | collective-permute-done | bytes 1048608 | tf_op jit(solution)/shard_map/ppermute | solution.py:65
  532.5 16.1 %collective-permute-done.32.refs_2_ = f32[4,64,1024]{2,1,0:T(8,128)S(1)} collective-permute-done((f32[4,64,1024]{2,1,0:T(8,128)}, f32[4,64,1024]{2,1,0:T(8,128)S(1)}, u32[]{:S(2)}, u32[]{:S(2)}) %collective-permute-start.32) | collective-permute-done | bytes 1048608 | tf_op jit(solution)/shard_map/ppermute | solution.py:65
  567.5 12.4 %shard_map.376 = f32[512,512]{1,0:T(8,128)} custom-call(s32[1]{0:T(128)} %bitcast.core_ref, f32[64,1024]{1,0:T(8,128)} %copy-done.18, bf16[1024,4096]{1,0:T(8,128)(2,1)} %weight_ref.7, f32[512,1024]{1,0:T(8,128)} %get-tuple-element.196.stream_ref), custom_call_target="tpu_custom_call" | custom-call | flops 1024 | bytes 1024 | tf_op jit(solution)/shard_map/pallas_call | solution.py:1076
  588.4 17.6 %all-to-all-done.7 = f32[4,64,1024]{2,1,0:T(8,128)S(1)} async-done(((f32[4,64,1024]{2,1,0:T(8,128)}), f32[4,64,1024]{2,1,0:T(8,128)S(1)}, u32[]{:S(2)}, u32[]{:S(2)}) %all-to-all-start.7) | async-done | bytes 1048608 | tf_op jit(solution)/shard_map/all_to_all | solution.py:90
  617.9 23.4 %collective-permute-done.33 = f32[64,2176]{1,0:T(8,128)} collective-permute-done((f32[64,2176]{1,0:T(8,128)}, f32[64,2176]{1,0:T(8,128)}, u32[]{:S(2)}, u32[]{:S(2)}) %collective-permute-start.33) | collective-permute-done | bytes 557088 | tf_op jit(solution)/shard_map/ppermute | solution.py:65
  644.6 9.1 %shard_map.377 = f32[64,4096]{1,0:T(8,128)} custom-call(f32[512,128]{1,0:T(8,128)} %bitcast.262, f32[512,4096]{1,0:T(8,128)} %all-gather.2.cloned.1.call-done.bytes_ref.refs_0_.refs_1_.refs_2_.refs_3_.refs_4_.refs_5_.refs_6_.refs_7_, f32[512,4096]{1,0:T(8,128)} %all-gather.2.cloned.1.call-done.bytes_ref.refs_0_.refs_1_.refs_2_.refs_3_.refs_4_.refs_5_.refs_6_.refs_7_, ...), custom_call_target="tpu_custom_call" | custom-call | flops 1024 | bytes 1024 | tf_op jit(solution)/shard_map/pallas_call | solution.py:347
  (429 shorter events, 297.6 us)
Async XLA Ops:
  7.2 291.4 %all-gather.2.cloned.1.call-start = ((), (), s32[]{:S(2)}) async-start(), calls=%async_computation.10 | async-start | bytes 9437184 | tf_op jit(solution)/shard_map/all_gather | solution.py:1215
  17.8 43.0 %collective-permute-start.1 = (f32[512,128]{1,0:T(8,128)}, f32[512,128]{1,0:T(8,128)}, u32[]{:S(2)}, u32[]{:S(2)}) collective-permute-start(f32[512,128]{1,0:T(8,128)} %bitcast_convert_fusion.own_ref), channel_id=1, source_target_pairs={{0,1},{1,0},{2,3},{3,2},{4,5},{5,4},{6,7},{7,6},{8,9},{9,8},{10,11... | collective-permute-start | bytes 786440 | tf_op jit(solution)/shard_map/ppermute | solution.py:65
  26.4 47.7 %all-to-all-start = ((f32[16,32,512]{2,1,0:T(8,128)}), f32[16,32,512]{2,1,0:T(8,128)S(1)}, u32[]{:S(2)}, u32[]{:S(2)}) async-start(f32[16,32,512]{2,1,0:T(8,128)} %select_maximum_fusion), calls=%async_computation | async-start | bytes 2097152 | tf_op jit(solution)/shard_map/all_to_all | solution.py:362
  155.2 143.4 %all-to-all-start.2 = ((f32[4,512,512]{2,1,0:T(8,128)}), f32[4,512,512]{2,1,0:T(8,128)}, u32[]{:S(2)}, u32[]{:S(2)}) async-start(f32[4,512,512]{2,1,0:T(8,128)} %broadcast_in_dim.70), calls=%async_computation.2 | async-start | bytes 8388608 | tf_op jit(solution)/shard_map/all_to_all | solution.py:90
  172.7 70.6 %collective-permute-start.10 = (f32[512,128]{1,0:T(8,128)}, f32[512,128]{1,0:T(8,128)S(1)}, u32[]{:S(2)}, u32[]{:S(2)}) collective-permute-start(f32[512,128]{1,0:T(8,128)} %bitcast_convert_fusion.own_ref), channel_id=1, source_target_pairs={{0,24},{2,26},{4,28},{6,30},{8,16},{10,18},{12,20},{14,22},{16,8},... | collective-permute-start | bytes 786440 | tf_op jit(solution)/shard_map/ppermute | solution.py:65
  176.6 105.3 %collective-permute-start.9 = (f32[512,128]{1,0:T(8,128)}, f32[512,128]{1,0:T(8,128)S(1)}, u32[]{:S(2)}, u32[]{:S(2)}) collective-permute-start(f32[512,128]{1,0:T(8,128)} %bitcast_convert_fusion.own_ref), channel_id=1, source_target_pairs={{0,16},{2,18},{4,20},{6,22},{8,24},{10,26},{12,28},{14,30},{16,0},... | collective-permute-start | bytes 786440 | tf_op jit(solution)/shard_map/ppermute | solution.py:65
  176.7 105.3 %collective-permute-start.8 = (f32[512,128]{1,0:T(8,128)}, f32[512,128]{1,0:T(8,128)S(1)}, u32[]{:S(2)}, u32[]{:S(2)}) collective-permute-start(f32[512,128]{1,0:T(8,128)} %bitcast_convert_fusion.own_ref), channel_id=1, source_target_pairs={{0,8},{2,10},{4,12},{6,14},{8,0},{10,2},{12,4},{14,6},{16,24},{18,... | collective-permute-start | bytes 786440 | tf_op jit(solution)/shard_map/ppermute | solution.py:65
  183.6 120.5 %collective-permute-start.5 = (f32[512,1024]{1,0:T(8,128)}, f32[512,1024]{1,0:T(8,128)}, u32[]{:S(2)}, u32[]{:S(2)}) collective-permute-start(f32[512,1024]{1,0:T(8,128)} %fusion.47), channel_id=1, source_target_pairs={{0,1},{1,0},{2,3},{3,2},{4,5},{5,4},{6,7},{7,6},{8,9},{9,8},{10,11... | collective-permute-start | bytes 6291464 | tf_op jit(solution)/shard_map/ppermute | solution.py:65
  332.5 57.1 %collective-permute-start.19 = (f32[2,4,64,1024]{3,2,1,0:T(8,128)}, f32[2,4,64,1024]{3,2,1,0:T(8,128)S(1)}, u32[]{:S(2)}, u32[]{:S(2)}) collective-permute-start(f32[2,4,64,1024]{3,2,1,0:T(8,128)} %get-tuple-element.127), channel_id=1, source_target_pairs={{0,2},{2,0},{4,6},{6,4},{8,10},{10,8},{12,14},{14,12},{16,18},{18,... | collective-permute-start | bytes 6291464 | tf_op jit(solution)/shard_map/ppermute | solution.py:65
  334.3 64.2 %collective-permute-start.20 = (f32[2,4,64,1152]{3,2,1,0:T(8,128)}, f32[2,4,64,1152]{3,2,1,0:T(8,128)}, u32[]{:S(2)}, u32[]{:S(2)}) collective-permute-start(f32[2,4,64,1152]{3,2,1,0:T(8,128)} %get-tuple-element.130), channel_id=1, source_target_pairs={{0,4},{2,6},{4,0},{6,2},{8,12},{10,14},{12,8},{14,10},{16,20},{18,... | collective-permute-start | bytes 7077896 | tf_op jit(solution)/shard_map/ppermute | solution.py:65
  346.3 78.0 %all-to-all-start.4 = ((f32[16,32,512]{2,1,0:T(8,128)}), f32[16,32,512]{2,1,0:T(8,128)S(1)}, u32[]{:S(2)}, u32[]{:S(2)}) async-start(f32[16,32,512]{2,1,0:T(8,128)} %bitcast.283), calls=%async_computation.4 | async-start | bytes 2097152 | tf_op jit(solution)/shard_map/all_to_all | solution.py:362
  350.2 54.5 %collective-permute-start.16 = (f32[64,1280]{1,0:T(8,128)}, f32[64,1280]{1,0:T(8,128)S(1)}, u32[]{:S(2)}, u32[]{:S(2)}) collective-permute-start(f32[64,1280]{1,0:T(8,128)} %get-tuple-element.219), channel_id=1, source_target_pairs={{0,8},{2,10},{4,12},{6,14},{8,0},{10,2},{12,4},{14,6},{16,24},{18,... | collective-permute-start | bytes 983048 | tf_op jit(solution)/shard_map/ppermute | solution.py:65
  398.5 82.4 %collective-permute-start.25 = (f32[2,4,64,1024]{3,2,1,0:T(8,128)}, f32[2,4,64,1024]{3,2,1,0:T(8,128)}, u32[]{:S(2)}, u32[]{:S(2)}) collective-permute-start(f32[2,4,64,1024]{3,2,1,0:T(8,128)} %get-tuple-element.138), channel_id=1, source_target_pairs={{0,2},{2,0},{4,6},{6,4},{8,10},{10,8},{12,14},{14,12},{16,18},{18,... | collective-permute-start | bytes 6291464 | tf_op jit(solution)/shard_map/ppermute | solution.py:65
  424.2 60.3 %collective-permute-start.26 = (f32[2,4,64,1024]{3,2,1,0:T(8,128)}, f32[2,4,64,1024]{3,2,1,0:T(8,128)S(1)}, u32[]{:S(2)}, u32[]{:S(2)}) collective-permute-start(f32[2,4,64,1024]{3,2,1,0:T(8,128)} %get-tuple-element.153), channel_id=1, source_target_pairs={{0,4},{2,6},{4,0},{6,2},{8,12},{10,14},{12,8},{14,10},{16,20},{18,... | collective-permute-start | bytes 6291464 | tf_op jit(solution)/shard_map/ppermute | solution.py:65
  439.6 49.8 %all-to-all-start.5 = ((f32[8,72,128]{2,1,0:T(8,128)}), f32[8,72,128]{2,1,0:T(8,128)S(1)}, u32[]{:S(2)}, u32[]{:S(2)}) async-start(f32[8,72,128]{2,1,0:T(8,128)} %pad_maximum_fusion.12), calls=%async_computation.5 | async-start | bytes 589824 | tf_op jit(solution)/shard_map/all_to_all | solution.py:1451
  476.2 51.6 %collective-permute-start.29 = (f32[4,64,1152]{2,1,0:T(8,128)}, f32[4,64,1152]{2,1,0:T(8,128)}, u32[]{:S(2)}, u32[]{:S(2)}) collective-permute-start(f32[4,64,1152]{2,1,0:T(8,128)} %shard_map.370), channel_id=1, source_target_pairs={{0,2},{2,0},{4,6},{6,4},{8,10},{10,8},{12,14},{14,12},{16,18},{18,... | collective-permute-start | bytes 3538952 | tf_op jit(solution)/shard_map/ppermute | solution.py:65
  500.2 48.4 %collective-permute-start.32 = (f32[4,64,1024]{2,1,0:T(8,128)}, f32[4,64,1024]{2,1,0:T(8,128)S(1)}, u32[]{:S(2)}, u32[]{:S(2)}) collective-permute-start(f32[4,64,1024]{2,1,0:T(8,128)} %shard_map.373), channel_id=1, source_target_pairs={{0,4},{2,6},{4,0},{6,2},{8,12},{10,14},{12,8},{14,10},{16,20},{18,... | collective-permute-start | bytes 3145736 | tf_op jit(solution)/shard_map/ppermute | solution.py:65
  503.7 49.7 %all-to-all-start.9 = ((f32[16,40,128]{2,1,0:T(8,128)}), f32[16,40,128]{2,1,0:T(8,128)S(1)}, u32[]{:S(2)}, u32[]{:S(2)}) async-start(f32[16,40,128]{2,1,0:T(8,128)} %broadcast_in_dim.73), calls=%async_computation.9 | async-start | bytes 655360 | tf_op jit(solution)/shard_map/all_to_all | solution.py:362
  553.3 52.7 %all-to-all-start.7 = ((f32[4,64,1024]{2,1,0:T(8,128)}), f32[4,64,1024]{2,1,0:T(8,128)S(1)}, u32[]{:S(2)}, u32[]{:S(2)}) async-start(f32[4,64,1024]{2,1,0:T(8,128)} %shard_map.380), calls=%async_computation.7 | async-start | bytes 2097152 | tf_op jit(solution)/shard_map/all_to_all | solution.py:90
  561.8 56.1 %collective-permute-start.34 = (f32[64,2176]{1,0:T(8,128)}, f32[64,2176]{1,0:T(8,128)}, u32[]{:S(2)}, u32[]{:S(2)}) collective-permute-start(f32[64,2176]{1,0:T(8,128)} %get-tuple-element.204), channel_id=1, source_target_pairs={{0,24},{2,26},{4,28},{6,30},{8,16},{10,18},{12,20},{14,22},{16,8},... | collective-permute-start | bytes 1671176 | tf_op jit(solution)/shard_map/ppermute | solution.py:65
  565.6 75.6 %collective-permute-start.33 = (f32[64,2176]{1,0:T(8,128)}, f32[64,2176]{1,0:T(8,128)}, u32[]{:S(2)}, u32[]{:S(2)}) collective-permute-start(f32[64,2176]{1,0:T(8,128)} %get-tuple-element.205), channel_id=1, source_target_pairs={{0,16},{2,18},{4,20},{6,22},{8,24},{10,26},{12,28},{14,30},{16,0},... | collective-permute-start | bytes 1671176 | tf_op jit(solution)/shard_map/ppermute | solution.py:65
  565.6 75.6 %collective-permute-start.31 = (f32[64,2176]{1,0:T(8,128)}, f32[64,2176]{1,0:T(8,128)}, u32[]{:S(2)}, u32[]{:S(2)}) collective-permute-start(f32[64,2176]{1,0:T(8,128)} %get-tuple-element.203), channel_id=1, source_target_pairs={{0,8},{2,10},{4,12},{6,14},{8,0},{10,2},{12,4},{14,6},{16,24},{18,... | collective-permute-start | bytes 1671176 | tf_op jit(solution)/shard_map/ppermute | solution.py:65
  566.2 47.6 %collective-permute-start.35 = (f32[2,4,64,384]{3,2,1,0:T(8,128)}, f32[2,4,64,384]{3,2,1,0:T(8,128)S(1)}, u32[]{:S(2)}, u32[]{:S(2)}) collective-permute-start(f32[2,4,64,384]{3,2,1,0:T(8,128)} %get-tuple-element.176), channel_id=1, source_target_pairs={{0,2},{2,0},{4,6},{6,4},{8,10},{10,8},{12,14},{14,12},{16,18},{18,... | collective-permute-start | bytes 2359304 | tf_op jit(solution)/shard_map/ppermute | solution.py:65
  606.0 51.1 %all-to-all-start.6 = ((f32[4,64,1024]{2,1,0:T(8,128)}), f32[4,64,1024]{2,1,0:T(8,128)S(1)}, u32[]{:S(2)}, u32[]{:S(2)}) async-start(f32[4,64,1024]{2,1,0:T(8,128)} %shard_map.379), calls=%async_computation.6 | async-start | bytes 2097152 | tf_op jit(solution)/shard_map/all_to_all | solution.py:90
  (91 other events, 1856.6 us)
Sparse Core Ops, SparseCore 0:
  17.2 177.9 all-gather.1
